TPU v7x, 256 devices: a whole 4x4x8 slice. The times are simulated.
256 devices in a mesh: island: 8 (over y, core), shard: 32 (over x, z).
Axes of the slice: x: 4, y: 4, z: 8, core: 2. Of those that a mesh axis runs over, the one named last changes fastest.
Arguments:
- pseudo_grad: float32 [8, 8192, 4096], P('island', 'shard'), may hold values from -6 to 6
- error_buffer: float32 [8, 8192, 4096], P('island', 'shard'), may hold values from -6 to 6
- momentum: float32 [8192, 4096], P('shard'), may hold values from -4 to 4
- weights: bfloat16 [8192, 4096], P('shard'), may hold values from -6 to 6
- warm_basis: float32 [8192, 64], P('shard'), may hold values from -6 to 6
Outputs:
- new_error: float32 [8, 8192, 4096], P('island', 'shard')
- new_momentum: float32 [8192, 4096], P('shard')
- new_weights: bfloat16 [8192, 4096], P('shard')
- new_basis: float32 [8192, 64], P('shard')
All inputs are finite; a program needn't handle non-finite values.
Results may differ from a plain program's by a relative error of at most 0.001.
Values sent between devices are 32-bit elements; how exact they have to be, the bound alone decides.
No kernel may reach another device: no remote copies, remote signals or barrier semaphores. Data moves between devices by JAX's collectives and lax.ppermute only.
A program may use at most 128 MiB of HBM per device.

v0:
```python
import jax
import jax.numpy as jnp
from jax import lax
from jax.experimental import pallas as pl
from jax.experimental.pallas import tpu as pltpu
from jax.sharding import Mesh, PartitionSpec as P

HIGHEST = lax.Precision.HIGHEST
F32, BF16 = jnp.float32, jnp.bfloat16
outer_beta = 0.9
outer_rate = 0.7
SIBLING = [(0, 1), (1, 0)]
LANES = 128
WIDE = 1024
PER = WIDE // LANES


def halves(value):
    high = value.astype(BF16)
    return high, (value - high.astype(F32)).astype(BF16)


def dot(a, b, dims=((1,), (0,)), precision=None):
    return lax.dot_general(a, b, (dims, ((), ())), precision=precision, preferred_element_type=F32)


def joined(blocks_ref):
    return jnp.concatenate([blocks_ref[j] for j in range(PER)], axis=1)


def put_blocks(out_ref, value):
    for j in range(PER):
        out_ref[j] = value[:, j * LANES : (j + 1) * LANES]


def rank_product(basis_t, high, low):
    basis_high, basis_low = halves(basis_t)
    ranks = basis_t.shape[0]
    both = dot(jnp.concatenate([basis_high, basis_low], axis=0), high)
    return both[:ranks] + both[ranks:] + dot(basis_high, low)


def stacked_columns(factor_t):
    high, low = halves(factor_t.T)
    return jnp.concatenate([high, low, high], axis=1)


def first_kernel(grad_ref, error_ref, basis_ref, high_ref, low_ref, partial_ref):
    high, low = halves(grad_ref[0] + error_ref[0])
    high_ref[...] = high
    low_ref[...] = low
    put_blocks(partial_ref, rank_product(basis_ref[...], high, low))


def partial_kernel(high_ref, low_ref, summed_ref, inverse_ref, partial_ref, basis_ref):
    @pl.when(pl.program_id(0) == 0)
    def _():
        basis_ref[...] = dot(inverse_ref[...], summed_ref[...], precision=HIGHEST)

    put_blocks(partial_ref, rank_product(basis_ref[...], high_ref[...], low_ref[...]))


def proj_kernel(factor_ref, high_ref, low_ref, out_ref):
    @pl.when(pl.program_id(0) == 0)
    def _():
        out_ref[...] = jnp.zeros_like(out_ref)

    high, low = halves(joined(factor_ref))
    ranks = high.shape[0]
    across = ((1,), (1,))
    both = dot(jnp.concatenate([high, low], axis=0), high_ref[...], across)
    out_ref[...] += both[:ranks] + both[ranks:] + dot(high, low_ref[...], across)


def error_kernel(high_ref, low_ref, factor_ref, proj_ref, inverse_ref, error_ref, rows_ref, left_ref):
    @pl.when(pl.program_id(0) == 0)
    def _():
        left_ref[...] = stacked_columns(dot(inverse_ref[...], proj_ref[...], precision=HIGHEST))

    high, low = halves(dot(inverse_ref[...], joined(factor_ref), precision=HIGHEST))
    rows = jnp.concatenate([high, high, low], axis=0)
    rows_ref[...] = rows
    merged = high_ref[...].astype(F32) + low_ref[...].astype(F32)
    error_ref[0] = merged - dot(left_ref[...], rows)


def step_kernel(rows_ref, momentum_ref, weights_ref, summed_ref, inverse_ref, new_momentum_ref, new_weights_ref, basis_ref, left_ref):
    @pl.when(pl.program_id(0) == 0)
    def _():
        basis = dot(inverse_ref[...], summed_ref[...], precision=HIGHEST)
        basis_ref[...] = basis
        left_ref[...] = stacked_columns(basis * 0.125)

    update = dot(left_ref[...], rows_ref[...])
    new_momentum = outer_beta * momentum_ref[...] + update
    new_momentum_ref[...] = new_momentum
    stepped = weights_ref[...].astype(F32) - outer_rate * (update + outer_beta * new_momentum)
    new_weights_ref[...] = stepped.astype(BF16)


def wide(rows):
    return pl.BlockSpec((rows, WIDE), lambda i: (0, i))


def whole(*shape):
    return pl.BlockSpec(shape, lambda i: (0,) * len(shape))


def replica(rows):
    return pl.BlockSpec((1, rows, WIDE), lambda i: (0, 0, i))


def blocks(ranks):
    return pl.BlockSpec((PER, ranks, LANES), lambda i: (i, 0, 0))


def call(kernel, columns, in_specs, outs, scratch=(), flops=0, traffic=0, limit=24):
    shapes = [jax.ShapeDtypeStruct(shape, kind) for shape, kind, _ in outs]
    specs = [spec for _, _, spec in outs]
    return pl.pallas_call(
        kernel,
        grid=(columns // WIDE,),
        in_specs=in_specs,
        out_shape=shapes,
        out_specs=specs,
        scratch_shapes=list(scratch),
        compiler_params=pltpu.CompilerParams(vmem_limit_bytes=limit * 2**20),
        cost_estimate=pl.CostEstimate(flops=flops, bytes_accessed=traffic, transcendentals=0),
    )


def at(pieces, index):
    return lax.dynamic_index_in_dim(pieces, index, 0, keepdims=False)


def around(axis, distance):
    size = lax.axis_size(axis)
    return [(i, (i + distance) % size) for i in range(size)]


def summed_directly(value, axis):
    size = lax.axis_size(axis)
    arrived = [lax.ppermute(value, axis, around(axis, d)) for d in range(1, size)]
    total = value
    for other in arrived:
        total = total + other
    return total


def to_everyone(piece, axes):
    size = lax.axis_size(axes)
    copies = jnp.broadcast_to(piece[None], (size, *piece.shape))
    return lax.all_to_all(copies, axes, 0, 0, tiled=True)


def summed_everywhere(pieces):
    count, ranks, width = pieces.shape
    core = lax.axis_index("core")
    pieces = pieces.reshape(2, count // 2, ranks, width)
    pieces = at(pieces, core) + lax.ppermute(at(pieces, 1 - core), "core", SIBLING)
    piece = lax.all_to_all(pieces, ("y", "x"), 0, 0, tiled=True).sum(axis=0)
    piece = to_everyone(piece, "z").sum(axis=0)
    pieces = to_everyone(piece, ("y", "x"))
    other = lax.ppermute(pieces, "core", SIBLING)
    out = jnp.zeros((2, *pieces.shape), pieces.dtype)
    out = lax.dynamic_update_index_in_dim(out, pieces, core, 0)
    out = lax.dynamic_update_index_in_dim(out, other, 1 - core, 0)
    return out.reshape(count, ranks, width)


def over_island(value):
    paired = summed_directly(value, "core")
    return paired, summed_directly(paired, "y")


def spread(tile, column):
    return jnp.broadcast_to(tile[:, column : column + 1], tile.shape)


def inverse_kernel(factor_ref, anchor_ref, out_ref):
    ranks = factor_ref.shape[1]
    gram = jnp.zeros((ranks, ranks), F32)
    for q in range(0, factor_ref.shape[0], 4):
        part = jnp.concatenate([factor_ref[q + j] for j in range(4)], axis=1)
        gram += dot(part, part, ((1,), (1,)), HIGHEST)
    row = lax.broadcasted_iota(jnp.int32, (ranks, ranks), 0)
    diagonal = row == lax.broadcasted_iota(jnp.int32, (ranks, ranks), 1)
    kept = jnp.where(diagonal, gram, 0.0)
    across = lax.rsqrt(jnp.sum(kept, axis=0, keepdims=True))
    down = lax.rsqrt(jnp.sum(kept, axis=1, keepdims=True))
    work = jnp.concatenate([gram * down * across, jnp.where(diagonal, across, 0.0)], axis=1)
    tiles = [work[8 * t : 8 * t + 8] for t in range(ranks // 8)]
    row = lax.broadcasted_iota(jnp.int32, (8, 2 * ranks), 0)
    out = []
    for j in range(0, ranks, 2):
        t, s = divmod(j, 8)
        left, right = spread(tiles[t], j), spread(tiles[t], j + 1)
        top, low = tiles[t][s : s + 1], tiles[t][s + 1 : s + 2]
        a, b, d = left[s : s + 1], left[s + 1 : s + 2], right[s + 1 : s + 2]
        det = a * d - b * b
        over = 1.0 / det
        rest = a * low - b * top
        first = (d * top - b * low) * over
        second = rest * over
        out.append(top * lax.rsqrt(a))
        out.append(rest * lax.rsqrt(a * det))
        for k in range(t, ranks // 8):
            if k > t:
                left, right = spread(tiles[k], j), spread(tiles[k], j + 1)
            elif s < 6:
                left = jnp.where(row > s + 1, left, 0.0)
                right = jnp.where(row > s + 1, right, 0.0)
            else:
                continue
            tiles[k] = tiles[k] - left * first - right * second
    out_ref[...] = jnp.concatenate(out, axis=0)[:, ranks:]


def inverse_factor(factor, anchor):
    ranks = factor.shape[1]
    return pl.pallas_call(
        inverse_kernel,
        in_specs=[pl.BlockSpec(memory_space=pltpu.VMEM), pl.BlockSpec(memory_space=pl.ANY)],
        out_shape=jax.ShapeDtypeStruct((ranks, ranks), F32),
        compiler_params=pltpu.CompilerParams(vmem_limit_bytes=8 * 2**20),
        cost_estimate=pl.CostEstimate(flops=2 * 10**9, bytes_accessed=2**21, transcendentals=0),
    )(factor, anchor)


def on_device(pseudo_grad, error_buffer, momentum, weights, warm_basis):
    _, rows, columns = pseudo_grad.shape
    ranks = warm_basis.shape[1]
    count = columns // LANES
    flops = 6 * rows * columns * ranks
    size = 4 * rows * columns
    half = ((rows, columns), BF16, wide(rows))
    partial_out = ((count, ranks, LANES), F32, blocks(ranks))
    short = whole(ranks, rows)
    square = whole(ranks, ranks)

    high, low, partial_blocks = call(
        first_kernel,
        columns,
        [replica(rows), replica(rows), short],
        [half, half, partial_out],
        flops=flops,
        traffic=3 * size,
        limit=56,
    )(pseudo_grad, error_buffer, warm_basis.T)
    project = call(
        proj_kernel,
        columns,
        [blocks(ranks), wide(rows), wide(rows)],
        [((ranks, rows), F32, short)],
        flops=flops,
        traffic=size,
    )
    factor = summed_everywhere(partial_blocks)
    (proj_t,) = project(factor, high, low)
    paired, summed_t = over_island(proj_t)
    inverse = inverse_factor(factor, paired)
    (partial_blocks,) = call(
        partial_kernel,
        columns,
        [wide(rows), wide(rows), short, square],
        [partial_out],
        [pltpu.VMEM((ranks, rows), F32)],
        flops=flops,
        traffic=size,
    )(high, low, summed_t, inverse)
    factor = summed_everywhere(partial_blocks)
    (proj_t,) = project(factor, high, low)
    paired, summed_t = over_island(proj_t)
    inverse = inverse_factor(factor, paired)
    new_error, factor_rows = call(
        error_kernel,
        columns,
        [wide(rows), wide(rows), blocks(ranks), short, square],
        [
            ((1, rows, columns), F32, replica(rows)),
            ((3 * ranks, columns), BF16, wide(3 * ranks)),
        ],
        [pltpu.VMEM((rows, 3 * ranks), BF16)],
        flops=flops,
        traffic=2 * size,
    )(high, low, factor, proj_t, inverse)
    new_momentum, new_weights, basis_t = call(
        step_kernel,
        columns,
        [wide(3 * ranks), wide(rows), wide(rows), short, square],
        [
            ((rows, columns), F32, wide(rows)),
            ((rows, columns), BF16, wide(rows)),
            ((ranks, rows), F32, short),
        ],
        [pltpu.VMEM((rows, 3 * ranks), BF16)],
        flops=flops,
        traffic=3 * size,
    )(factor_rows, momentum, weights, summed_t, inverse)
    return new_error, new_momentum, new_weights, basis_t.T


def solution(mesh):
    grid = Mesh(mesh.devices.reshape(4, 2, 4, 8), ("y", "core", "x", "z"))
    island, shard = ("y", "core"), ("x", "z")
    in_specs = (
        P(island, shard, None),
        P(island, shard, None),
        P(shard, None),
        P(shard, None),
        P(shard, None),
    )
    out_specs = (P(island, shard, None), P(shard, None), P(shard, None), P(shard, None))
    return jax.shard_map(
        on_device, mesh=grid, in_specs=in_specs, out_specs=out_specs, check_vma=False
    )
```

profile of v0, /device:TPU:1, one launch (start us, length us, event | category | flops | bytes accessed | tf_op | source)
XLA Modules:
  0.0 145.4 jit_solution(14271984106024911731)
XLA Ops:
  0.6 6.1 %shard_map.84 = (bf16[256,4096]{1,0:T(8,128)(2,1)}, bf16[256,4096]{1,0:T(8,128)(2,1)}, f32[32,64,128]{2,1,0:T(8,128)}) custom-call(f32[1,256,4096]{2,1,0:T(8,128)} %grad_ref.1, f32[1,256,4096]{2,1,0:T(8,128)} %error_ref.1, f32[64,256]{1,0:T(8,128)} %bitcast.31), custom_call_target="tpu_custom_call" | custom-call | flops 402653184 | bytes 12582912 | tf_op jit(solution)/shard_map/pallas_call | solution.py:241
  6.7 1.1 dynamic-slice_bitcast_fusion.1
  7.8 3.3 %collective-permute-start = (f32[16,64,128]{2,1,0:T(8,128)S(1)}, f32[16,64,128]{2,1,0:T(8,128)S(1)}, u32[]{:S(2)}, u32[]{:S(2)}) collective-permute-start(f32[16,64,128]{2,1,0:T(8,128)S(1)} %dynamic-slice_bitcast_fusion.1), channel_id=1, source_target_pairs={{0,32},{32,0},{1,33},{33,1},{2,34},{34,2},{3,35},{35,3},{4,36},{36... | collective-permute-start | bytes 1572872 | tf_op jit(solution)/shard_map/ppermute | solution.py:160
  11.2 1.5 %collective-permute-done = f32[16,64,128]{2,1,0:T(8,128)S(1)} collective-permute-done((f32[16,64,128]{2,1,0:T(8,128)S(1)}, f32[16,64,128]{2,1,0:T(8,128)S(1)}, u32[]{:S(2)}, u32[]{:S(2)}) %collective-permute-start) | collective-permute-done | bytes 524320 | tf_op jit(solution)/shard_map/ppermute | solution.py:160
  12.7 1.9 %bitcast_add_fusion.1 = f32[16,64,128]{2,1,0:T(8,128)} fusion(f32[16,64,128]{2,1,0:T(8,128)S(1)} %collective-permute-done, f32[2,16,64,128]{3,2,1,0:T(8,128)} %bitcast.30, s32[]{:T(128)S(6)} %select_n.14), kind=kLoop, calls=%fused_computation.5 | loop fusion | flops 131072 | bytes 1572868 | tf_op jit(solution)/shard_map/add | solution.py:160
  14.6 5.0 %all-to-all-start = ((f32[16,64,128]{2,1,0:T(8,128)}), f32[16,64,128]{2,1,0:T(8,128)S(1)}, u32[]{:S(2)}, u32[]{:S(2)}) async-start(f32[16,64,128]{2,1,0:T(8,128)} %bitcast_add_fusion.1), calls=%async_computation | async-start | bytes 1048576 | tf_op jit(solution)/shard_map/all_to_all | solution.py:161
  19.6 10.7 %all-to-all-done = f32[16,64,128]{2,1,0:T(8,128)S(1)} async-done(((f32[16,64,128]{2,1,0:T(8,128)}), f32[16,64,128]{2,1,0:T(8,128)S(1)}, u32[]{:S(2)}, u32[]{:S(2)}) %all-to-all-start) | async-done | bytes 524320 | tf_op jit(solution)/shard_map/all_to_all | solution.py:161
  30.4 17.2 %all_to_all.32 = f32[8,64,128]{2,1,0:T(8,128)S(1)} all-to-all(f32[8,64,128]{2,1,0:T(8,128)S(1)} %broadcast_in_dim.37), channel_id=1, replica_groups=mesh['y'=4,'core'=2,'x'=4,'z'=8] {'z'}, dimensions={0} | all-to-all | bytes 524288 | tf_op jit(solution)/shard_map/all_to_all | solution.py:153
  47.6 13.4 %all_to_all.30 = f32[16,64,128]{2,1,0:T(8,128)S(1)} all-to-all(f32[16,64,128]{2,1,0:T(8,128)S(1)} %broadcast_in_dim.38), channel_id=1, replica_groups=mesh['y'=4,'core'=2,'x'=4,'z'=8] {'y','x'}, dimensions={0} | all-to-all | bytes 1048576 | tf_op jit(solution)/shard_map/all_to_all | solution.py:153
  61.0 4.1 %collective-permute-start.1 = (f32[16,64,128]{2,1,0:T(8,128)S(1)}, f32[16,64,128]{2,1,0:T(8,128)S(1)}, u32[]{:S(2)}, u32[]{:S(2)}) collective-permute-start(f32[16,64,128]{2,1,0:T(8,128)S(1)} %all_to_all.30), channel_id=1, source_target_pairs={{0,32},{32,0},{1,33},{33,1},{2,34},{34,2},{3,35},{35,3},{4,36},{36... | collective-permute-start | bytes 1572872 | tf_op jit(solution)/shard_map/ppermute | solution.py:164
  65.3 1.4 collective-permute-done.1
  66.7 2.2 %shard_map.85 = f32[64,256]{1,0:T(8,128)S(1)} custom-call(f32[32,64,128]{2,1,0:T(8,128)S(1)} %bitcast.27, bf16[256,4096]{1,0:T(8,128)(2,1)S(1)} %copy-done, bf16[256,4096]{1,0:T(8,128)(2,1)S(1)} %copy-done.1), custom_call_target="tpu_custom_call" | custom-call | flops 402653184 | bytes 4194304 | tf_op jit(solution)/shard_map/pallas_call | solution.py:259
  69.3 0.9 collective-permute-done.2
  70.3 0.7 collective-permute-start.5
  70.9 0.7 collective-permute-start.4
  71.8 4.2 %shard_map.86.inverse_ref = f32[64,64]{1,0:T(8,128)S(1)} custom-call(f32[32,64,128]{2,1,0:T(8,128)S(1)} %bitcast.28, f32[64,256]{1,0:T(8,128)S(1)} %add.48.anchor_ref), custom_call_target="tpu_custom_call" | custom-call | flops 2000000000 | bytes 2097152 | tf_op jit(solution)/shard_map/pallas_call | solution.py:221
  76.0 1.3 collective-permute-done.3
  77.3 1.7 %shard_map.87 = f32[32,64,128]{2,1,0:T(8,128)S(1)} custom-call(bf16[256,4096]{1,0:T(8,128)(2,1)S(1)} %copy-done, bf16[256,4096]{1,0:T(8,128)(2,1)S(1)} %copy-done.1, f32[64,256]{1,0:T(8,128)S(1)} %add_add_fusion.1.summed_ref, f32[64,64]{1,0:T(8,128)S(1)} %shard_map.86.inverse_ref), custom_call_target="tpu_custom_call" | custom-call | flops 402653184 | bytes 4194304 | tf_op jit(solution)/shard_map/pallas_call | solution.py:262
  79.1 1.1 collective-permute-start.6
  80.2 1.5 %collective-permute-done.6 = f32[16,64,128]{2,1,0:T(8,128)S(1)} collective-permute-done((f32[16,64,128]{2,1,0:T(8,128)S(1)}, f32[16,64,128]{2,1,0:T(8,128)S(1)}, u32[]{:S(2)}, u32[]{:S(2)}) %collective-permute-start.6) | collective-permute-done | bytes 524320 | tf_op jit(solution)/shard_map/ppermute | solution.py:160
  81.8 14.6 %all_to_all.33 = f32[16,64,128]{2,1,0:T(8,128)S(1)} all-to-all(f32[16,64,128]{2,1,0:T(8,128)S(1)} %bitcast_add_fusion), channel_id=1, replica_groups=mesh['y'=4,'core'=2,'x'=4,'z'=8] {'y','x'}, dimensions={0} | all-to-all | bytes 1048576 | tf_op jit(solution)/shard_map/all_to_all | solution.py:161
  96.5 11.9 %all_to_all.34 = f32[8,64,128]{2,1,0:T(8,128)S(1)} all-to-all(f32[8,64,128]{2,1,0:T(8,128)S(1)} %broadcast_in_dim.41), channel_id=1, replica_groups=mesh['y'=4,'core'=2,'x'=4,'z'=8] {'z'}, dimensions={0} | all-to-all | bytes 524288 | tf_op jit(solution)/shard_map/all_to_all | solution.py:153
  108.5 13.0 %all_to_all.31 = f32[16,64,128]{2,1,0:T(8,128)S(1)} all-to-all(f32[16,64,128]{2,1,0:T(8,128)S(1)} %broadcast_in_dim.42), channel_id=1, replica_groups=mesh['y'=4,'core'=2,'x'=4,'z'=8] {'y','x'}, dimensions={0} | all-to-all | bytes 1048576 | tf_op jit(solution)/shard_map/all_to_all | solution.py:153
  121.5 4.1 %collective-permute-start.7 = (f32[16,64,128]{2,1,0:T(8,128)S(1)}, f32[16,64,128]{2,1,0:T(8,128)S(1)}, u32[]{:S(2)}, u32[]{:S(2)}) collective-permute-start(f32[16,64,128]{2,1,0:T(8,128)S(1)} %all_to_all.31), channel_id=1, source_target_pairs={{0,32},{32,0},{1,33},{33,1},{2,34},{34,2},{3,35},{35,3},{4,36},{36... | collective-permute-start | bytes 1572872 | tf_op jit(solution)/shard_map/ppermute | solution.py:164
  125.8 1.4 collective-permute-done.7
  127.2 2.2 %shard_map.88.proj_ref = f32[64,256]{1,0:T(8,128)S(1)} custom-call(f32[32,64,128]{2,1,0:T(8,128)S(1)} %bitcast.22, bf16[256,4096]{1,0:T(8,128)(2,1)S(1)} %copy-done, bf16[256,4096]{1,0:T(8,128)(2,1)S(1)} %copy-done.2), custom_call_target="tpu_custom_call" | custom-call | flops 402653184 | bytes 4194304 | tf_op jit(solution)/shard_map/pallas_call | solution.py:272
  129.9 0.9 collective-permute-done.8
  130.8 0.7 collective-permute-start.11
  131.4 0.7 collective-permute-start.10
  132.3 4.2 %shard_map.89.inverse_ref = f32[64,64]{1,0:T(8,128)S(1)} custom-call(f32[32,64,128]{2,1,0:T(8,128)S(1)} %bitcast.23, f32[64,256]{1,0:T(8,128)S(1)} %add.53.anchor_ref), custom_call_target="tpu_custom_call" | custom-call | flops 2000000000 | bytes 2097152 | tf_op jit(solution)/shard_map/pallas_call | solution.py:221
  136.5 4.4 %shard_map.90 = (f32[1,256,4096]{2,1,0:T(8,128)}, bf16[192,4096]{1,0:T(8,128)(2,1)S(1)}) custom-call(bf16[256,4096]{1,0:T(8,128)(2,1)S(1)} %copy-done, bf16[256,4096]{1,0:T(8,128)(2,1)S(1)} %copy-done.2, f32[32,64,128]{2,1,0:T(8,128)S(1)} %bitcast.24, f32[64,256]{1,0:T(8,128)S(1)} %shard_map.88.proj_ref, f32[64,64]{1,0:T(8,128)S(1)} %shard_map.89.inverse_ref), custom_call_target="tpu_custom_call" | custom-call | flops 402653184 | bytes 8388608 | tf_op jit(solution)/shard_map/pallas_call | solution.py:275
  141.0 4.4 %shard_map.91 = (f32[256,4096]{1,0:T(8,128)}, bf16[256,4096]{1,0:T(8,128)(2,1)}, f32[64,256]{1,0:T(8,128)}) custom-call(bf16[192,4096]{1,0:T(8,128)(2,1)S(1)} %get-tuple-element.16.rows_ref, f32[256,4096]{1,0:T(8,128)S(1)} %copy-done.3, bf16[256,4096]{1,0:T(8,128)(2,1)S(1)} %copy-done.4, f32[64,256]{1,0:T(8,128)S(1)} %add_add_fusion.summed_ref, ...), custom_call_target="tpu_custom_call" | custom-call | flops 402653184 | bytes 12582912 | tf_op jit(solution)/shard_map/pallas_call | solution.py:287
  (39 shorter events, 2.2 us)
Async XLA Ops:
  7.8 4.9 %collective-permute-start = (f32[16,64,128]{2,1,0:T(8,128)S(1)}, f32[16,64,128]{2,1,0:T(8,128)S(1)}, u32[]{:S(2)}, u32[]{:S(2)}) collective-permute-start(f32[16,64,128]{2,1,0:T(8,128)S(1)} %dynamic-slice_bitcast_fusion.1), channel_id=1, source_target_pairs={{0,32},{32,0},{1,33},{33,1},{2,34},{34,2},{3,35},{35,3},{4,36},{36... | collective-permute-start | bytes 1572872 | tf_op jit(solution)/shard_map/ppermute | solution.py:160
  11.2 55.5 %copy-start = (bf16[256,4096]{1,0:T(8,128)(2,1)S(1)}, bf16[256,4096]{1,0:T(8,128)(2,1)}, u32[]{:S(2)}) copy-start(bf16[256,4096]{1,0:T(8,128)(2,1)} %get-tuple-element.12.high_ref) | copy-start | bytes 6291460
  14.6 15.7 %all-to-all-start = ((f32[16,64,128]{2,1,0:T(8,128)}), f32[16,64,128]{2,1,0:T(8,128)S(1)}, u32[]{:S(2)}, u32[]{:S(2)}) async-start(f32[16,64,128]{2,1,0:T(8,128)} %bitcast_add_fusion.1), calls=%async_computation | async-start | bytes 1048576 | tf_op jit(solution)/shard_map/all_to_all | solution.py:161
  47.6 19.1 %copy-start.1 = (bf16[256,4096]{1,0:T(8,128)(2,1)S(1)}, bf16[256,4096]{1,0:T(8,128)(2,1)}, u32[]{:S(2)}) copy-start(bf16[256,4096]{1,0:T(8,128)(2,1)} %get-tuple-element.13.low_ref) | copy-start | bytes 6291460
  61.0 5.6 %collective-permute-start.1 = (f32[16,64,128]{2,1,0:T(8,128)S(1)}, f32[16,64,128]{2,1,0:T(8,128)S(1)}, u32[]{:S(2)}, u32[]{:S(2)}) collective-permute-start(f32[16,64,128]{2,1,0:T(8,128)S(1)} %all_to_all.30), channel_id=1, source_target_pairs={{0,32},{32,0},{1,33},{33,1},{2,34},{34,2},{3,35},{35,3},{4,36},{36... | collective-permute-start | bytes 1572872 | tf_op jit(solution)/shard_map/ppermute | solution.py:164
  68.9 1.4 collective-permute-start.2
  70.3 5.7 %collective-permute-start.5 = (f32[64,256]{1,0:T(8,128)S(1)}, f32[64,256]{1,0:T(8,128)S(1)}, u32[]{:S(2)}, u32[]{:S(2)}) collective-permute-start(f32[64,256]{1,0:T(8,128)S(1)} %add.48.anchor_ref), channel_id=1, source_target_pairs={{0,192},{64,0},{128,64},{192,128},{1,193},{65,1},{129,65},{193,129... | collective-permute-start | bytes 196616 | tf_op jit(solution)/shard_map/ppermute | solution.py:143
  70.9 5.1 %collective-permute-start.4 = (f32[64,256]{1,0:T(8,128)S(1)}, f32[64,256]{1,0:T(8,128)S(1)}, u32[]{:S(2)}, u32[]{:S(2)}) collective-permute-start(f32[64,256]{1,0:T(8,128)S(1)} %add.48.anchor_ref), channel_id=1, source_target_pairs={{0,128},{64,192},{128,0},{192,64},{1,129},{65,193},{129,1},{193,65... | collective-permute-start | bytes 196616 | tf_op jit(solution)/shard_map/ppermute | solution.py:143
  71.6 5.7 %collective-permute-start.3 = (f32[64,256]{1,0:T(8,128)S(1)}, f32[64,256]{1,0:T(8,128)S(1)}, u32[]{:S(2)}, u32[]{:S(2)}) collective-permute-start(f32[64,256]{1,0:T(8,128)S(1)} %add.48.anchor_ref), channel_id=1, source_target_pairs={{0,64},{64,128},{128,192},{192,0},{1,65},{65,129},{129,193},{193,1... | collective-permute-start | bytes 196616 | tf_op jit(solution)/shard_map/ppermute | solution.py:143
  79.1 2.6 %collective-permute-start.6 = (f32[16,64,128]{2,1,0:T(8,128)S(1)}, f32[16,64,128]{2,1,0:T(8,128)S(1)}, u32[]{:S(2)}, u32[]{:S(2)}) collective-permute-start(f32[16,64,128]{2,1,0:T(8,128)S(1)} %dynamic-slice_bitcast_fusion), channel_id=1, source_target_pairs={{0,32},{32,0},{1,33},{33,1},{2,34},{34,2},{3,35},{35,3},{4,36},{36... | collective-permute-start | bytes 1572872 | tf_op jit(solution)/shard_map/ppermute | solution.py:160
  108.5 18.8 %copy-start.2 = (bf16[256,4096]{1,0:T(8,128)(2,1)S(1)}, bf16[256,4096]{1,0:T(8,128)(2,1)}, u32[]{:S(2)}) copy-start(bf16[256,4096]{1,0:T(8,128)(2,1)} %get-tuple-element.13.low_ref) | copy-start | bytes 6291460
  121.5 5.6 %collective-permute-start.7 = (f32[16,64,128]{2,1,0:T(8,128)S(1)}, f32[16,64,128]{2,1,0:T(8,128)S(1)}, u32[]{:S(2)}, u32[]{:S(2)}) collective-permute-start(f32[16,64,128]{2,1,0:T(8,128)S(1)} %all_to_all.31), channel_id=1, source_target_pairs={{0,32},{32,0},{1,33},{33,1},{2,34},{34,2},{3,35},{35,3},{4,36},{36... | collective-permute-start | bytes 1572872 | tf_op jit(solution)/shard_map/ppermute | solution.py:164
  129.4 1.4 collective-permute-start.8
  130.8 10.1 %collective-permute-start.11 = (f32[64,256]{1,0:T(8,128)S(1)}, f32[64,256]{1,0:T(8,128)S(1)}, u32[]{:S(2)}, u32[]{:S(2)}) collective-permute-start(f32[64,256]{1,0:T(8,128)S(1)} %add.53.anchor_ref), channel_id=1, source_target_pairs={{0,192},{64,0},{128,64},{192,128},{1,193},{65,1},{129,65},{193,129... | collective-permute-start | bytes 196616 | tf_op jit(solution)/shard_map/ppermute | solution.py:143
  131.4 9.5 %collective-permute-start.10 = (f32[64,256]{1,0:T(8,128)S(1)}, f32[64,256]{1,0:T(8,128)S(1)}, u32[]{:S(2)}, u32[]{:S(2)}) collective-permute-start(f32[64,256]{1,0:T(8,128)S(1)} %add.53.anchor_ref), channel_id=1, source_target_pairs={{0,128},{64,192},{128,0},{192,64},{1,129},{65,193},{129,1},{193,65... | collective-permute-start | bytes 196616 | tf_op jit(solution)/shard_map/ppermute | solution.py:143
  132.1 8.8 %collective-permute-start.9 = (f32[64,256]{1,0:T(8,128)S(1)}, f32[64,256]{1,0:T(8,128)S(1)}, u32[]{:S(2)}, u32[]{:S(2)}) collective-permute-start(f32[64,256]{1,0:T(8,128)S(1)} %add.53.anchor_ref), channel_id=1, source_target_pairs={{0,64},{64,128},{128,192},{192,0},{1,65},{65,129},{129,193},{193,1... | collective-permute-start | bytes 196616 | tf_op jit(solution)/shard_map/ppermute | solution.py:143
  132.3 8.6 %copy-start.4 = (bf16[256,4096]{1,0:T(8,128)(2,1)S(1)}, bf16[256,4096]{1,0:T(8,128)(2,1)}, u32[]{:S(2)}) copy-start(bf16[256,4096]{1,0:T(8,128)(2,1)} %weights_ref.1) | copy-start | bytes 6291460
  136.5 4.5 %copy-start.3 = (f32[256,4096]{1,0:T(8,128)S(1)}, f32[256,4096]{1,0:T(8,128)}, u32[]{:S(2)}) copy-start(f32[256,4096]{1,0:T(8,128)} %momentum_ref.1) | copy-start | bytes 12582916
where the time goes:
time: 146 us; the launch traced here: 145 us
  blocking collectives  70.1 us (48%)
  Pallas kernels  29.3 us (20%)
  starting transfers between devices  21.7 us (15%)
  waiting for transfers between devices  19.6 us (13%)
  other arithmetic  2.13 us (1%)
  local copies, waits for them, and re-layouts  1.67 us (1%)
    all_to_all x4, blocking collectives, to_everyone(): return lax.all_to_all(copies, axes, 0, 0, tiled=True)  55.5 us
    all_to_all x1, blocking collectives, summed_everywhere(): piece = lax.all_to_all(pieces, ('y', 'x'), 0, 0, tiled=True).sum(axis=0)  14.6 us
    all_to_all x1, waiting for transfers between devices, summed_everywhere(): piece = lax.all_to_all(pieces, ('y', 'x'), 0, 0, tiled=True).sum(axis=0)  10.7 us
    pallas_call x2, Pallas kernels, inverse_factor(): pl.pallas_call(inverse_kernel, in_specs=[pl.BlockSpec(memory_space=pltpu....  8.36 us
    ppermute x2, starting transfers between devices, summed_everywhere(): other = lax.ppermute(pieces, 'core', SIBLING)  8.2 us
    pallas_call x1, Pallas kernels, on_device(): call(first_kernel, columns, [replica(rows), replica(rows), short], [half,...  6.11 us
    all_to_all x1, starting transfers between devices, summed_everywhere(): piece = lax.all_to_all(pieces, ('y', 'x'), 0, 0, tiled=True).sum(axis=0)  5.02 us
    ppermute x2, starting transfers between devices, summed_everywhere(): lax.ppermute(at(pieces, 1 - core), 'core', SIBLING)  4.43 us
  transfers between devices with their start and end apart: 13, of which 8 were waited for; matrix products, arithmetic and copies ran while one was open for 0% of the time, Pallas kernels for 9%

commit v1 on v0

--- a/solution.py
+++ b/solution.py
@@ -13,6 +13,7 @@
 LANES = 128
 WIDE = 1024
 PER = WIDE // LANES
+CHUNK = 512
 
 
 def halves(value):
@@ -45,11 +46,60 @@
     return jnp.concatenate([high, low, high], axis=1)
 
 
-def first_kernel(grad_ref, error_ref, basis_ref, high_ref, low_ref, partial_ref):
-    high, low = halves(grad_ref[0] + error_ref[0])
-    high_ref[...] = high
-    low_ref[...] = low
-    put_blocks(partial_ref, rank_product(basis_ref[...], high, low))
+def first_kernel(grad_ref, error_ref, basis_ref, high_ref, low_ref, away_ref, kept_ref, given_ref, grads, errors, highs, lows, basis, sems):
+    columns = grad_ref.shape[2]
+    count = columns // CHUNK
+    core = lax.axis_index("core")
+    start = pltpu.make_async_copy(basis_ref, basis, sems.at[5, 0])
+    start.start()
+    copies = []
+    for c in range(count):
+        here = slice(c * CHUNK, (c + 1) * CHUNK)
+        pair = [
+            pltpu.make_async_copy(source.at[0, :, here], target.at[:, here], sems.at[i, c])
+            for i, (source, target) in enumerate(((grad_ref, grads), (error_ref, errors)))
+        ]
+        for copy in pair:
+            copy.start()
+        copies.append(pair)
+    leaving = []
+    start.wait()
+    for c, pair in enumerate(copies):
+        here = slice(c * CHUNK, (c + 1) * CHUNK)
+        for copy in pair:
+            copy.wait()
+        merged = grads[:, here] + errors[:, here]
+        high, low = halves(merged)
+        highs[:, here] = high
+        lows[:, here] = low
+        grads[:, here] = merged
+        for i, (source, target) in enumerate(((highs, high_ref), (lows, low_ref))):
+            copy = pltpu.make_async_copy(source.at[:, here], target.at[:, here], sems.at[2 + i, c])
+            copy.start()
+            leaving.append(copy)
+        partial = rank_product(basis[...], high, low)
+        side, place = divmod(c, count // 2)
+        there = slice(place * CHUNK, (place + 1) * CHUNK)
+        first = place * (CHUNK // LANES)
+
+        def put(ref):
+            for j in range(CHUNK // LANES):
+                ref[first + j] = partial[:, j * LANES : (j + 1) * LANES]
+
+        @pl.when(core == side)
+        def _():
+            put(kept_ref)
+
+        @pl.when(core != side)
+        def _():
+            put(given_ref)
+            pltpu.make_async_copy(grads.at[:, here], away_ref.at[:, there], sems.at[4, place]).start()
+
+    for copy in leaving:
+        copy.wait()
+    for place in range(count // 2):
+        there = slice(place * CHUNK, (place + 1) * CHUNK)
+        pltpu.make_async_copy(grads.at[:, there], away_ref.at[:, there], sems.at[4, place]).wait()
 
 
 def partial_kernel(high_ref, low_ref, summed_ref, inverse_ref, partial_ref, basis_ref):
@@ -60,16 +110,36 @@
     put_blocks(partial_ref, rank_product(basis_ref[...], high_ref[...], low_ref[...]))
 
 
-def proj_kernel(factor_ref, high_ref, low_ref, out_ref):
+def add_projection(factor, high, low, out_ref, gram_ref):
     @pl.when(pl.program_id(0) == 0)
     def _():
         out_ref[...] = jnp.zeros_like(out_ref)
-
-    high, low = halves(joined(factor_ref))
-    ranks = high.shape[0]
+        gram_ref[...] = jnp.zeros_like(gram_ref)
+
     across = ((1,), (1,))
-    both = dot(jnp.concatenate([high, low], axis=0), high_ref[...], across)
-    out_ref[...] += both[:ranks] + both[ranks:] + dot(high, low_ref[...], across)
+    factor_high, factor_low = halves(factor)
+    ranks = factor.shape[0]
+    both = dot(jnp.concatenate([factor_high, factor_low], axis=0), high, across)
+    out_ref[...] += both[:ranks] + both[ranks:] + dot(factor_high, low, across)
+    gram_ref[...] += dot(factor, factor, across, HIGHEST)
+
+
+def paired_kernel(core_ref, factor_ref, high_ref, low_ref, arrived_ref, out_ref, high_out, low_out, gram_ref):
+    merged = high_ref[...].astype(F32) + low_ref[...].astype(F32)
+    high, low = halves(merged + arrived_ref[...])
+    high_out[...] = high
+    low_out[...] = low
+    rows = high.shape[0]
+    ranks = factor_ref.shape[1]
+    add_projection(joined(factor_ref), high, low, out_ref.at[:, :rows], gram_ref)
+
+    @pl.when(pl.program_id(0) == pl.num_programs(0) - 1)
+    def _():
+        out_ref[:, rows:] = jnp.concatenate([gram_ref[...], jnp.zeros((ranks, LANES - ranks), F32)], axis=1)
+
+
+def proj_kernel(factor_ref, high_ref, low_ref, out_ref, gram_ref):
+    add_projection(joined(factor_ref), high_ref[...], low_ref[...], out_ref, gram_ref)
 
 
 def error_kernel(high_ref, low_ref, factor_ref, proj_ref, inverse_ref, error_ref, rows_ref, left_ref):
@@ -129,10 +199,6 @@
     )
 
 
-def at(pieces, index):
-    return lax.dynamic_index_in_dim(pieces, index, 0, keepdims=False)
-
-
 def around(axis, distance):
     size = lax.axis_size(axis)
     return [(i, (i + distance) % size) for i in range(size)]
@@ -153,36 +219,28 @@
     return lax.all_to_all(copies, axes, 0, 0, tiled=True)
 
 
-def summed_everywhere(pieces):
-    count, ranks, width = pieces.shape
-    core = lax.axis_index("core")
-    pieces = pieces.reshape(2, count // 2, ranks, width)
-    pieces = at(pieces, core) + lax.ppermute(at(pieces, 1 - core), "core", SIBLING)
+def over_chips(pieces):
     piece = lax.all_to_all(pieces, ("y", "x"), 0, 0, tiled=True).sum(axis=0)
     piece = to_everyone(piece, "z").sum(axis=0)
-    pieces = to_everyone(piece, ("y", "x"))
+    return to_everyone(piece, ("y", "x"))
+
+
+def both_halves(pieces):
+    core = lax.axis_index("core")
     other = lax.ppermute(pieces, "core", SIBLING)
     out = jnp.zeros((2, *pieces.shape), pieces.dtype)
     out = lax.dynamic_update_index_in_dim(out, pieces, core, 0)
     out = lax.dynamic_update_index_in_dim(out, other, 1 - core, 0)
-    return out.reshape(count, ranks, width)
-
-
-def over_island(value):
-    paired = summed_directly(value, "core")
-    return paired, summed_directly(paired, "y")
+    return out.reshape(-1, *pieces.shape[1:])
 
 
 def spread(tile, column):
     return jnp.broadcast_to(tile[:, column : column + 1], tile.shape)
 
 
-def inverse_kernel(factor_ref, anchor_ref, out_ref):
-    ranks = factor_ref.shape[1]
-    gram = jnp.zeros((ranks, ranks), F32)
-    for q in range(0, factor_ref.shape[0], 4):
-        part = jnp.concatenate([factor_ref[q + j] for j in range(4)], axis=1)
-        gram += dot(part, part, ((1,), (1,)), HIGHEST)
+def inverse_kernel(gram_ref, anchor_ref, out_ref):
+    ranks = out_ref.shape[0]
+    gram = gram_ref[:, :ranks]
     row = lax.broadcasted_iota(jnp.int32, (ranks, ranks), 0)
     diagonal = row == lax.broadcasted_iota(jnp.int32, (ranks, ranks), 1)
     kept = jnp.where(diagonal, gram, 0.0)
@@ -216,15 +274,72 @@
     out_ref[...] = jnp.concatenate(out, axis=0)[:, ranks:]
 
 
-def inverse_factor(factor, anchor):
-    ranks = factor.shape[1]
+def inverse_factor(gram, anchor, block=0):
+    ranks, width = gram.shape
     return pl.pallas_call(
         inverse_kernel,
-        in_specs=[pl.BlockSpec(memory_space=pltpu.VMEM), pl.BlockSpec(memory_space=pl.ANY)],
+        grid=(1,),
+        in_specs=[
+            pl.BlockSpec((ranks, min(width, LANES)), lambda i: (0, block)),
+            pl.BlockSpec(memory_space=pl.ANY),
+        ],
+        out_specs=pl.BlockSpec((ranks, ranks), lambda i: (0, 0)),
         out_shape=jax.ShapeDtypeStruct((ranks, ranks), F32),
         compiler_params=pltpu.CompilerParams(vmem_limit_bytes=8 * 2**20),
-        cost_estimate=pl.CostEstimate(flops=2 * 10**9, bytes_accessed=2**21, transcendentals=0),
-    )(factor, anchor)
+        cost_estimate=pl.CostEstimate(flops=2 * 10**9, bytes_accessed=2**20, transcendentals=0),
+    )(gram, anchor)
+
+
+def first_product(pseudo_grad, error_buffer, basis_t):
+    _, rows, columns = pseudo_grad.shape
+    ranks = basis_t.shape[0]
+    count = columns // LANES // 2
+    in_vmem = pl.BlockSpec(memory_space=pltpu.VMEM)
+    in_hbm = pl.BlockSpec(memory_space=pltpu.HBM)
+    part = jax.ShapeDtypeStruct((count, ranks, LANES), F32)
+    half = pltpu.HBM((rows, columns), BF16)
+    return pl.pallas_call(
+        first_kernel,
+        in_specs=[in_hbm] * 3,
+        out_shape=[half, half, pltpu.HBM((rows, columns // 2), F32), part, part],
+        out_specs=[in_hbm] * 3 + [in_vmem] * 2,
+        scratch_shapes=[
+            pltpu.VMEM((rows, columns), F32),
+            pltpu.VMEM((rows, columns), F32),
+            pltpu.VMEM((rows, columns), BF16),
+            pltpu.VMEM((rows, columns), BF16),
+            pltpu.VMEM((ranks, rows), F32),
+            pltpu.SemaphoreType.DMA((6, columns // CHUNK)),
+        ],
+        compiler_params=pltpu.CompilerParams(vmem_limit_bytes=24 * 2**20),
+        cost_estimate=pl.CostEstimate(
+            flops=6 * rows * columns * ranks, bytes_accessed=12 * rows * columns, transcendentals=0
+        ),
+    )(*(pltpu.with_memory_space_constraint(x, pltpu.HBM) for x in (pseudo_grad, error_buffer, basis_t)))
+
+
+def paired_product(core, factor, high, low, arrived):
+    count, ranks, _ = factor.shape
+    rows, half = arrived.shape
+    steps = half // WIDE
+    mine = pl.BlockSpec((rows, WIDE), lambda i, core: (0, core[0] * steps + i))
+    here = pl.BlockSpec((rows, WIDE), lambda i, core: (0, i))
+    share = jax.ShapeDtypeStruct((rows, half), BF16)
+    return pl.pallas_call(
+        paired_kernel,
+        grid_spec=pltpu.PrefetchScalarGridSpec(
+            num_scalar_prefetch=1,
+            grid=(steps,),
+            in_specs=[pl.BlockSpec((PER, ranks, LANES), lambda i, core: (i, 0, 0)), mine, mine, here],
+            out_specs=[pl.BlockSpec((ranks, rows + LANES), lambda i, core: (0, 0)), here, here],
+            scratch_shapes=[pltpu.VMEM((ranks, ranks), F32)],
+        ),
+        out_shape=[jax.ShapeDtypeStruct((ranks, rows + LANES), F32), share, share],
+        compiler_params=pltpu.CompilerParams(vmem_limit_bytes=24 * 2**20),
+        cost_estimate=pl.CostEstimate(
+            flops=6 * rows * half * ranks, bytes_accessed=12 * rows * half, transcendentals=0
+        ),
+    )(core, factor, high, pltpu.with_memory_space_constraint(low, pltpu.HBM), arrived)
 
 
 def on_device(pseudo_grad, error_buffer, momentum, weights, warm_basis):
@@ -233,45 +348,40 @@
     count = columns // LANES
     flops = 6 * rows * columns * ranks
     size = 4 * rows * columns
-    half = ((rows, columns), BF16, wide(rows))
-    partial_out = ((count, ranks, LANES), F32, blocks(ranks))
     short = whole(ranks, rows)
     square = whole(ranks, ranks)
-
-    high, low, partial_blocks = call(
-        first_kernel,
-        columns,
-        [replica(rows), replica(rows), short],
-        [half, half, partial_out],
-        flops=flops,
-        traffic=3 * size,
-        limit=56,
-    )(pseudo_grad, error_buffer, warm_basis.T)
-    project = call(
+    core = lax.axis_index("core").astype(jnp.int32).reshape(1)
+
+    high, low, away, kept, given = first_product(pseudo_grad, error_buffer, warm_basis.T)
+    kept = kept + lax.ppermute(given, "core", SIBLING)
+    kept, away = lax.optimization_barrier((kept, away))
+    arrived = lax.ppermute(away, "core", SIBLING)
+    factor = over_chips(kept)
+    proj_t, high_half, low_half = paired_product(core, factor, high, low, arrived)
+    paired = summed_directly(proj_t, "core")
+    summed_t = summed_directly(paired[:, :rows], "y")
+    inverse = inverse_factor(paired, paired, rows // LANES)
+    (partial_blocks,) = call(
+        partial_kernel,
+        columns // 2,
+        [wide(rows), wide(rows), short, square],
+        [((count // 2, ranks, LANES), F32, blocks(ranks))],
+        [pltpu.VMEM((ranks, rows), F32)],
+        flops=flops // 2,
+        traffic=size // 2,
+    )(high_half, low_half, summed_t, inverse)
+    factor = both_halves(over_chips(partial_blocks))
+    proj_t, gram = call(
         proj_kernel,
         columns,
         [blocks(ranks), wide(rows), wide(rows)],
-        [((ranks, rows), F32, short)],
+        [((ranks, rows), F32, short), ((ranks, ranks), F32, square)],
         flops=flops,
         traffic=size,
-    )
-    factor = summed_everywhere(partial_blocks)
-    (proj_t,) = project(factor, high, low)
-    paired, summed_t = over_island(proj_t)
-    inverse = inverse_factor(factor, paired)
-    (partial_blocks,) = call(
-        partial_kernel,
-        columns,
-        [wide(rows), wide(rows), short, square],
-        [partial_out],
-        [pltpu.VMEM((ranks, rows), F32)],
-        flops=flops,
-        traffic=size,
-    )(high, low, summed_t, inverse)
-    factor = summed_everywhere(partial_blocks)
-    (proj_t,) = project(factor, high, low)
-    paired, summed_t = over_island(proj_t)
-    inverse = inverse_factor(factor, paired)
+    )(factor, high, low)
+    paired = summed_directly(proj_t, "core")
+    summed_t = summed_directly(paired, "y")
+    inverse = inverse_factor(gram, paired)
     new_error, factor_rows = call(
         error_kernel,
         columns,

time: 146 us -> 139 us (0.952)
  waiting for transfers between devices: 19.6 us -> 14.7 us
  other arithmetic: 2.13 us -> 0.24 us
    all_to_all x1 -> x2, blocking collectives: 14.6 us -> 29.9 us  [over_chips(): piece = lax.all_to_all(pieces, ('y', 'x'), 0, 0, tiled=True).sum(axis=0)]
    all_to_all x4 -> x3, blocking collectives: 55.5 us -> 41 us  [to_everyone(): return lax.all_to_all(copies, axes, 0, 0, tiled=True)]
    ppermute x8, starting transfers between devices: 4.01 us -> 8.38 us  [summed_directly(): lax.ppermute(value, axis, around(axis, d))]
    ppermute x4 -> x3, starting transfers between devices: 12.6 us -> 8.29 us  [the longest x1 4.85 us: both_halves(): other = lax.ppermute(pieces, 'core', SIBLING)]
    ppermute x4 -> x3, waiting for transfers between devices: 5.8 us -> 2.9 us  [the longest x1 1.54 us: on_device(): kept = kept + lax.ppermute(given, 'core', SIBLING)]
    add x2 -> x1, other arithmetic: 1.97 us -> 0.08 us  [on_device(): kept = kept + lax.ppermute(given, 'core', SIBLING)]
    all_to_all x1, waiting for transfers between devices: 10.7 us -> 8.99 us  [to_everyone(): return lax.all_to_all(copies, axes, 0, 0, tiled=True)]
  transfers between devices with their start and end apart: 13 -> 12, of which waited for: 8 -> 6; matrix products, arithmetic and copies ran while one was open for 0% -> 1% of each run, Pallas kernels for 9% -> 8%
where the time goes in v1:
time: 139 us; the launch traced here: 138 us
  blocking collectives  70.9 us (51%)
  Pallas kernels  29.4 us (21%)
  starting transfers between devices  20.8 us (15%)
  waiting for transfers between devices  14.7 us (11%)
    all_to_all x3, blocking collectives, to_everyone(): return lax.all_to_all(copies, axes, 0, 0, tiled=True)  41 us
    all_to_all x2, blocking collectives, over_chips(): piece = lax.all_to_all(pieces, ('y', 'x'), 0, 0, tiled=True).sum(axis=0)  29.9 us
    all_to_all x1, waiting for transfers between devices, to_everyone(): return lax.all_to_all(copies, axes, 0, 0, tiled=True)  8.99 us
    ppermute x8, starting transfers between devices, summed_directly(): lax.ppermute(value, axis, around(axis, d))  8.38 us
    pallas_call x2, Pallas kernels, inverse_factor(): pl.pallas_call(inverse_kernel, grid=(1,), in_specs=[pl.BlockSpec((ranks,...  6.46 us
    pallas_call x1, Pallas kernels, first_product(): pl.pallas_call(first_kernel, in_specs=[in_hbm] * 3, out_shape=[half, half...  6.41 us
    ppermute x1, starting transfers between devices, both_halves(): other = lax.ppermute(pieces, 'core', SIBLING)  4.85 us
    pallas_call x1, Pallas kernels, on_device(): call(step_kernel, columns, [wide(3 * ranks), wide(rows), wide(rows), shor...  4.4 us
  transfers between devices with their start and end apart: 12, of which 6 were waited for; matrix products, arithmetic and copies ran while one was open for 1% of the time, Pallas kernels for 8%

profile of v1, /device:TPU:1, one launch (start us, length us, event | category | flops | bytes accessed | tf_op | source)
XLA Modules:
  0.0 138.0 jit_solution(15615337897887914738)
XLA Ops:
  0.6 6.4 %shard_map.84 = (bf16[256,4096]{1,0:T(8,128)(2,1)}, bf16[256,4096]{1,0:T(8,128)(2,1)}, f32[256,2048]{1,0:T(8,128)}, f32[16,64,128]{2,1,0:T(8,128)S(1)}, f32[16,64,128]{2,1,0:T(8,128)S(1)}) custom-call(f32[1,256,4096]{2,1,0:T(8,128)} %grad_ref.1, f32[1,256,4096]{2,1,0:T(8,128)} %error_ref.1, f32[64,256]{1,0:T(8,128)} %bitcast.10), custom_call_target="tpu_custom_call" | custom-call | flops 402653184 | bytes 12582912 | tf_op jit(solution)/shard_map/pallas_call | solution.py:301
  7.0 3.0 %collective-permute-start = (f32[16,64,128]{2,1,0:T(8,128)S(1)}, f32[16,64,128]{2,1,0:T(8,128)S(1)}, u32[]{:S(2)}, u32[]{:S(2)}) collective-permute-start(f32[16,64,128]{2,1,0:T(8,128)S(1)} %get-tuple-element.24), channel_id=1, source_target_pairs={{0,32},{32,0},{1,33},{33,1},{2,34},{34,2},{3,35},{35,3},{4,36},{36... | collective-permute-start | bytes 1572872 | tf_op jit(solution)/shard_map/ppermute | solution.py:356
  10.0 1.5 %collective-permute-done = f32[16,64,128]{2,1,0:T(8,128)S(1)} collective-permute-done((f32[16,64,128]{2,1,0:T(8,128)S(1)}, f32[16,64,128]{2,1,0:T(8,128)S(1)}, u32[]{:S(2)}, u32[]{:S(2)}) %collective-permute-start) | collective-permute-done | bytes 524320 | tf_op jit(solution)/shard_map/ppermute | solution.py:356
  11.7 0.5 collective-permute-start.1
  12.1 15.8 %all_to_all.30 = f32[16,64,128]{2,1,0:T(8,128)S(1)} all-to-all(f32[16,64,128]{2,1,0:T(8,128)S(1)} %add.35), channel_id=1, replica_groups=mesh['y'=4,'core'=2,'x'=4,'z'=8] {'y','x'}, dimensions={0} | all-to-all | bytes 1048576 | tf_op jit(solution)/shard_map/all_to_all | solution.py:223
  28.0 17.2 %all_to_all.31 = f32[8,64,128]{2,1,0:T(8,128)S(1)} all-to-all(f32[8,64,128]{2,1,0:T(8,128)S(1)} %broadcast_in_dim.17), channel_id=1, replica_groups=mesh['y'=4,'core'=2,'x'=4,'z'=8] {'z'}, dimensions={0} | all-to-all | bytes 524288 | tf_op jit(solution)/shard_map/all_to_all | solution.py:219
  45.2 0.9 broadcast_in_dim.36
  46.1 4.2 %all-to-all-start.2 = ((f32[16,64,128]{2,1,0:T(8,128)}), f32[16,64,128]{2,1,0:T(8,128)S(1)}, u32[]{:S(2)}, u32[]{:S(2)}) async-start(f32[16,64,128]{2,1,0:T(8,128)} %broadcast_in_dim.36), calls=%async_computation.2 | async-start | bytes 1048576 | tf_op jit(solution)/shard_map/all_to_all | solution.py:219
  50.3 9.0 %all-to-all-done.2.factor_ref = f32[16,64,128]{2,1,0:T(8,128)S(1)} async-done(((f32[16,64,128]{2,1,0:T(8,128)}), f32[16,64,128]{2,1,0:T(8,128)S(1)}, u32[]{:S(2)}, u32[]{:S(2)}) %all-to-all-start.2) | async-done | bytes 524320 | tf_op jit(solution)/shard_map/all_to_all | solution.py:219
  59.3 3.6 %shard_map.85 = (f32[64,384]{1,0:T(8,128)S(1)}, bf16[256,2048]{1,0:T(8,128)(2,1)S(1)}, bf16[256,2048]{1,0:T(8,128)(2,1)S(1)}) custom-call(s32[1]{0:T(128)} %bitcast.1.core_ref, f32[16,64,128]{2,1,0:T(8,128)S(1)} %all-to-all-done.2.factor_ref, bf16[256,4096]{1,0:T(8,128)(2,1)S(1)} %copy-done, bf16[256,4096]{1,0:T(8,128)(2,1)} %get-tuple-element.22.low_ref, ...), custom_call_target="tpu_custom_call" | custom-call | flops 201326592 | bytes 6291456 | tf_op jit(solution)/shard_map/pallas_call | solution.py:328
  62.8 4.3 %collective-permute-start.2 = (f32[64,384]{1,0:T(8,128)S(1)}, f32[64,384]{1,0:T(8,128)S(1)}, u32[]{:S(2)}, u32[]{:S(2)}) collective-permute-start(f32[64,384]{1,0:T(8,128)S(1)} %get-tuple-element.30), channel_id=1, source_target_pairs={{0,32},{32,0},{1,33},{33,1},{2,34},{34,2},{3,35},{35,3},{4,36},{36... | collective-permute-start | bytes 294920 | tf_op jit(solution)/shard_map/ppermute | solution.py:209
  67.1 0.9 collective-permute-done.2
  68.1 0.7 collective-permute-start.4
  68.7 1.3 collective-permute-start.5
  70.0 0.2 collective-permute-start.3
  70.2 3.2 %shard_map.86.inverse_ref = f32[64,64]{1,0:T(8,128)S(1)} custom-call(f32[64,384]{1,0:T(8,128)S(1)} %add.36.gram_ref.anchor_ref, f32[64,384]{1,0:T(8,128)S(1)} %add.36.gram_ref.anchor_ref), custom_call_target="tpu_custom_call" | custom-call | flops 2000000000 | bytes 1048576 | tf_op jit(solution)/shard_map/pallas_call | solution.py:279
  73.4 0.9 collective-permute-done.3
  74.4 1.0 shard_map.87
  75.4 14.1 %all_to_all.32 = f32[16,64,128]{2,1,0:T(8,128)S(1)} all-to-all(f32[16,64,128]{2,1,0:T(8,128)S(1)} %shard_map.87), channel_id=1, replica_groups=mesh['y'=4,'core'=2,'x'=4,'z'=8] {'y','x'}, dimensions={0} | all-to-all | bytes 1048576 | tf_op jit(solution)/shard_map/all_to_all | solution.py:223
  89.5 11.8 %all_to_all.33 = f32[8,64,128]{2,1,0:T(8,128)S(1)} all-to-all(f32[8,64,128]{2,1,0:T(8,128)S(1)} %broadcast_in_dim.37), channel_id=1, replica_groups=mesh['y'=4,'core'=2,'x'=4,'z'=8] {'z'}, dimensions={0} | all-to-all | bytes 524288 | tf_op jit(solution)/shard_map/all_to_all | solution.py:219
  101.4 11.9 %all_to_all.34 = f32[16,64,128]{2,1,0:T(8,128)S(1)} all-to-all(f32[16,64,128]{2,1,0:T(8,128)S(1)} %broadcast_in_dim.38), channel_id=1, replica_groups=mesh['y'=4,'core'=2,'x'=4,'z'=8] {'y','x'}, dimensions={0} | all-to-all | bytes 1048576 | tf_op jit(solution)/shard_map/all_to_all | solution.py:219
  113.3 4.9 %collective-permute-start.6 = (f32[16,64,128]{2,1,0:T(8,128)S(1)}, f32[16,64,128]{2,1,0:T(8,128)S(1)}, u32[]{:S(2)}, u32[]{:S(2)}) collective-permute-start(f32[16,64,128]{2,1,0:T(8,128)S(1)} %all_to_all.34), channel_id=1, source_target_pairs={{0,32},{32,0},{1,33},{33,1},{2,34},{34,2},{3,35},{35,3},{4,36},{36... | collective-permute-start | bytes 1572872 | tf_op jit(solution)/shard_map/ppermute | solution.py:230
  118.3 1.4 collective-permute-done.6
  119.8 3.2 %shard_map.88 = (f32[64,256]{1,0:T(8,128)S(1)}, f32[64,64]{1,0:T(8,128)S(1)}) custom-call(f32[32,64,128]{2,1,0:T(8,128)S(1)} %bitcast.8, bf16[256,4096]{1,0:T(8,128)(2,1)S(1)} %copy-done, bf16[256,4096]{1,0:T(8,128)(2,1)S(1)} %copy-done.1), custom_call_target="tpu_custom_call" | custom-call | flops 402653184 | bytes 4194304 | tf_op jit(solution)/shard_map/pallas_call | solution.py:374
  123.0 0.5 collective-permute-start.7
  123.5 0.9 collective-permute-done.7
  124.4 0.7 collective-permute-start.10
  125.0 0.7 collective-permute-start.9
  125.8 0.2 collective-permute-start.8
  125.9 3.2 %shard_map.89.inverse_ref = f32[64,64]{1,0:T(8,128)S(1)} custom-call(f32[64,64]{1,0:T(8,128)S(1)} %get-tuple-element.32.gram_ref, f32[64,256]{1,0:T(8,128)S(1)} %add.42.anchor_ref), custom_call_target="tpu_custom_call" | custom-call | flops 2000000000 | bytes 1048576 | tf_op jit(solution)/shard_map/pallas_call | solution.py:279
  129.2 4.4 %shard_map.90 = (f32[1,256,4096]{2,1,0:T(8,128)}, bf16[192,4096]{1,0:T(8,128)(2,1)S(1)}) custom-call(bf16[256,4096]{1,0:T(8,128)(2,1)S(1)} %copy-done, bf16[256,4096]{1,0:T(8,128)(2,1)S(1)} %copy-done.1, f32[32,64,128]{2,1,0:T(8,128)S(1)} %bitcast.9, f32[64,256]{1,0:T(8,128)S(1)} %get-tuple-element.31.proj_ref, f32[64,64]{1,0:T(8,128)S(1)} %shard_map.89.inverse_ref), custom_call_target="tpu_custom_call" | custom-call | flops 402653184 | bytes 8388608 | tf_op jit(solution)/shard_map/pallas_call | solution.py:385
  133.6 4.4 %shard_map.91 = (f32[256,4096]{1,0:T(8,128)}, bf16[256,4096]{1,0:T(8,128)(2,1)}, f32[64,256]{1,0:T(8,128)}) custom-call(bf16[192,4096]{1,0:T(8,128)(2,1)S(1)} %get-tuple-element.34.rows_ref, f32[256,4096]{1,0:T(8,128)S(1)} %copy-done.2, bf16[256,4096]{1,0:T(8,128)(2,1)S(1)} %copy-done.3, f32[64,256]{1,0:T(8,128)S(1)} %add_add_fusion.summed_ref, ...), custom_call_target="tpu_custom_call" | custom-call | flops 402653184 | bytes 12582912 | tf_op jit(solution)/shard_map/pallas_call | solution.py:397
  (30 shorter events, 0.6 us)
Async XLA Ops:
  7.0 4.5 %collective-permute-start = (f32[16,64,128]{2,1,0:T(8,128)S(1)}, f32[16,64,128]{2,1,0:T(8,128)S(1)}, u32[]{:S(2)}, u32[]{:S(2)}) collective-permute-start(f32[16,64,128]{2,1,0:T(8,128)S(1)} %get-tuple-element.24), channel_id=1, source_target_pairs={{0,32},{32,0},{1,33},{33,1},{2,34},{34,2},{3,35},{35,3},{4,36},{36... | collective-permute-start | bytes 1572872 | tf_op jit(solution)/shard_map/ppermute | solution.py:356
  11.6 47.6 %copy-start = (bf16[256,4096]{1,0:T(8,128)(2,1)S(1)}, bf16[256,4096]{1,0:T(8,128)(2,1)}, u32[]{:S(2)}) copy-start(bf16[256,4096]{1,0:T(8,128)(2,1)} %get-tuple-element.21.high_ref) | copy-start | bytes 6291460
  11.7 47.6 %collective-permute-start.1 = (f32[256,2048]{1,0:T(8,128)}, f32[256,2048]{1,0:T(8,128)}, u32[]{:S(2)}, u32[]{:S(2)}) collective-permute-start(f32[256,2048]{1,0:T(8,128)} %get-tuple-element.27), channel_id=1, source_target_pairs={{0,32},{32,0},{1,33},{33,1},{2,34},{34,2},{3,35},{35,3},{4,36},{36... | collective-permute-start | bytes 6291464 | tf_op jit(solution)/shard_map/ppermute | solution.py:358
  46.1 13.2 %all-to-all-start.2 = ((f32[16,64,128]{2,1,0:T(8,128)}), f32[16,64,128]{2,1,0:T(8,128)S(1)}, u32[]{:S(2)}, u32[]{:S(2)}) async-start(f32[16,64,128]{2,1,0:T(8,128)} %broadcast_in_dim.36), calls=%async_computation.2 | async-start | bytes 1048576 | tf_op jit(solution)/shard_map/all_to_all | solution.py:219
  62.8 5.2 %collective-permute-start.2 = (f32[64,384]{1,0:T(8,128)S(1)}, f32[64,384]{1,0:T(8,128)S(1)}, u32[]{:S(2)}, u32[]{:S(2)}) collective-permute-start(f32[64,384]{1,0:T(8,128)S(1)} %get-tuple-element.30), channel_id=1, source_target_pairs={{0,32},{32,0},{1,33},{33,1},{2,34},{34,2},{3,35},{35,3},{4,36},{36... | collective-permute-start | bytes 294920 | tf_op jit(solution)/shard_map/ppermute | solution.py:209
  68.1 5.4 %collective-permute-start.4 = (f32[64,256]{1,0:T(8,128)S(1)}, f32[64,256]{1,0:T(8,128)S(1)}, u32[]{:S(2)}, u32[]{:S(2)}) collective-permute-start(f32[64,256]{1,0:T(8,128)S(1)} %slice.4), channel_id=1, source_target_pairs={{0,128},{64,192},{128,0},{192,64},{1,129},{65,193},{129,1},{193,65... | collective-permute-start | bytes 196616 | tf_op jit(solution)/shard_map/ppermute | solution.py:209
  68.7 4.7 %collective-permute-start.5 = (f32[64,256]{1,0:T(8,128)S(1)}, f32[64,256]{1,0:T(8,128)S(1)}, u32[]{:S(2)}, u32[]{:S(2)}) collective-permute-start(f32[64,256]{1,0:T(8,128)S(1)} %slice.4), channel_id=1, source_target_pairs={{0,192},{64,0},{128,64},{192,128},{1,193},{65,1},{129,65},{193,129... | collective-permute-start | bytes 196616 | tf_op jit(solution)/shard_map/ppermute | solution.py:209
  70.0 4.3 %collective-permute-start.3 = (f32[64,256]{1,0:T(8,128)S(1)}, f32[64,256]{1,0:T(8,128)S(1)}, u32[]{:S(2)}, u32[]{:S(2)}) collective-permute-start(f32[64,256]{1,0:T(8,128)S(1)} %slice.4), channel_id=1, source_target_pairs={{0,64},{64,128},{128,192},{192,0},{1,65},{65,129},{129,193},{193,1... | collective-permute-start | bytes 196616 | tf_op jit(solution)/shard_map/ppermute | solution.py:209
  113.3 6.4 %collective-permute-start.6 = (f32[16,64,128]{2,1,0:T(8,128)S(1)}, f32[16,64,128]{2,1,0:T(8,128)S(1)}, u32[]{:S(2)}, u32[]{:S(2)}) collective-permute-start(f32[16,64,128]{2,1,0:T(8,128)S(1)} %all_to_all.34), channel_id=1, source_target_pairs={{0,32},{32,0},{1,33},{33,1},{2,34},{34,2},{3,35},{35,3},{4,36},{36... | collective-permute-start | bytes 1572872 | tf_op jit(solution)/shard_map/ppermute | solution.py:230
  118.2 1.6 %copy-start.1 = (bf16[256,4096]{1,0:T(8,128)(2,1)S(1)}, bf16[256,4096]{1,0:T(8,128)(2,1)}, u32[]{:S(2)}) copy-start(bf16[256,4096]{1,0:T(8,128)(2,1)} %get-tuple-element.22.low_ref) | copy-start | bytes 6291460
  123.0 1.4 collective-permute-start.7
  124.4 9.2 %collective-permute-start.10 = (f32[64,256]{1,0:T(8,128)S(1)}, f32[64,256]{1,0:T(8,128)S(1)}, u32[]{:S(2)}, u32[]{:S(2)}) collective-permute-start(f32[64,256]{1,0:T(8,128)S(1)} %add.42.anchor_ref), channel_id=1, source_target_pairs={{0,192},{64,0},{128,64},{192,128},{1,193},{65,1},{129,65},{193,129... | collective-permute-start | bytes 196616 | tf_op jit(solution)/shard_map/ppermute | solution.py:209
  125.0 8.5 %collective-permute-start.9 = (f32[64,256]{1,0:T(8,128)S(1)}, f32[64,256]{1,0:T(8,128)S(1)}, u32[]{:S(2)}, u32[]{:S(2)}) collective-permute-start(f32[64,256]{1,0:T(8,128)S(1)} %add.42.anchor_ref), channel_id=1, source_target_pairs={{0,128},{64,192},{128,0},{192,64},{1,129},{65,193},{129,1},{193,65... | collective-permute-start | bytes 196616 | tf_op jit(solution)/shard_map/ppermute | solution.py:209
  125.8 7.8 %collective-permute-start.8 = (f32[64,256]{1,0:T(8,128)S(1)}, f32[64,256]{1,0:T(8,128)S(1)}, u32[]{:S(2)}, u32[]{:S(2)}) collective-permute-start(f32[64,256]{1,0:T(8,128)S(1)} %add.42.anchor_ref), channel_id=1, source_target_pairs={{0,64},{64,128},{128,192},{192,0},{1,65},{65,129},{129,193},{193,1... | collective-permute-start | bytes 196616 | tf_op jit(solution)/shard_map/ppermute | solution.py:209
  125.9 7.7 %copy-start.3 = (bf16[256,4096]{1,0:T(8,128)(2,1)S(1)}, bf16[256,4096]{1,0:T(8,128)(2,1)}, u32[]{:S(2)}) copy-start(bf16[256,4096]{1,0:T(8,128)(2,1)} %weights_ref.1) | copy-start | bytes 6291460
  129.2 4.5 %copy-start.2 = (f32[256,4096]{1,0:T(8,128)S(1)}, f32[256,4096]{1,0:T(8,128)}, u32[]{:S(2)}) copy-start(f32[256,4096]{1,0:T(8,128)} %momentum_ref.1) | copy-start | bytes 12582916

commit v2 on v1

v2 whole, which is shorter than its diff:
```python
import functools

import jax
import jax.numpy as jnp
from jax import lax
from jax.experimental import pallas as pl
from jax.experimental.pallas import tpu as pltpu
from jax.sharding import Mesh, PartitionSpec as P

HIGHEST = lax.Precision.HIGHEST
F32, BF16 = jnp.float32, jnp.bfloat16
outer_beta = 0.9
outer_rate = 0.7
SIBLING = [(0, 1), (1, 0)]
LANES = 128
WIDE = 1024
PER = WIDE // LANES
CHUNK = 512


def halves(value):
    high = value.astype(BF16)
    return high, (value - high.astype(F32)).astype(BF16)


def dot(a, b, dims=((1,), (0,)), precision=None):
    return lax.dot_general(a, b, (dims, ((), ())), precision=precision, preferred_element_type=F32)


def joined(blocks_ref):
    return jnp.concatenate([blocks_ref[j] for j in range(PER)], axis=1)


def chunk_of(blocks_ref, c):
    per = CHUNK // LANES
    return jnp.concatenate([blocks_ref[c * per + j] for j in range(per)], axis=1)


def put_blocks(out_ref, value):
    for j in range(PER):
        out_ref[j] = value[:, j * LANES : (j + 1) * LANES]


def rank_product(basis_t, high, low):
    basis_high, basis_low = halves(basis_t)
    ranks = basis_t.shape[0]
    both = dot(jnp.concatenate([basis_high, basis_low], axis=0), high)
    return both[:ranks] + both[ranks:] + dot(basis_high, low)


def stacked_columns(factor_t):
    high, low = halves(factor_t.T)
    return jnp.concatenate([high, low, high], axis=1)


def column(side, place, columns):
    return pl.ds(pl.multiple_of(side * (columns // 2) + place * CHUNK, CHUNK), CHUNK)


def side_of(own):
    core = lax.axis_index("core")
    return core if own else 1 - core


def merge_kernel(own, grad_ref, error_ref, basis_ref, anchor_ref, merged_ref, partial_ref, grads, errors, basis, sems):
    columns = grad_ref.shape[2]
    count = columns // 2 // CHUNK
    side = side_of(own)
    start = pltpu.make_async_copy(basis_ref, basis, sems.at[2, count])
    start.start()
    copies = []
    for c in range(count):
        here = slice(c * CHUNK, (c + 1) * CHUNK)
        pair = [
            pltpu.make_async_copy(source.at[0, :, column(side, c, columns)], target.at[:, here], sems.at[i, c])
            for i, (source, target) in enumerate(((grad_ref, grads), (error_ref, errors)))
        ]
        for copy in pair:
            copy.start()
        copies.append(pair)
    leaving = []
    start.wait()
    for c, pair in enumerate(copies):
        here = slice(c * CHUNK, (c + 1) * CHUNK)
        for copy in pair:
            copy.wait()
        merged = grads[:, here] + errors[:, here]
        grads[:, here] = merged
        copy = pltpu.make_async_copy(grads.at[:, here], merged_ref.at[:, here], sems.at[2, c])
        copy.start()
        leaving.append(copy)
        partial = rank_product(basis[...], *halves(merged))
        for j in range(CHUNK // LANES):
            partial_ref[c * (CHUNK // LANES) + j] = partial[:, j * LANES : (j + 1) * LANES]
    for copy in leaving:
        copy.wait()


def partial_kernel(high_ref, low_ref, summed_ref, inverse_ref, partial_ref, basis_ref):
    @pl.when(pl.program_id(0) == 0)
    def _():
        basis_ref[...] = dot(inverse_ref[...], summed_ref[...], precision=HIGHEST)

    put_blocks(partial_ref, rank_product(basis_ref[...], high_ref[...], low_ref[...]))


ACROSS = ((1,), (1,))


def added_projection(totals, factor, high, low):
    both, rest, gram = totals
    ranks = factor.shape[0]
    factor_high, factor_low = halves(factor)
    last = (factor - factor_high.astype(F32) - factor_low.astype(F32)).astype(BF16)
    parts = jnp.concatenate([factor_high, factor_low, last], axis=0)
    return (
        both + dot(parts[: 2 * ranks], high, ACROSS),
        rest + dot(factor_high, low, ACROSS),
        gram + dot(parts, parts, ACROSS),
    )


def no_totals(ranks, rows):
    return (
        jnp.zeros((2 * ranks, rows), F32),
        jnp.zeros((ranks, rows), F32),
        jnp.zeros((3 * ranks, 3 * ranks), F32),
    )


def closed(totals):
    both, rest, gram = totals
    ranks = rest.shape[0]
    gram = gram[:ranks] + (gram[ranks : 2 * ranks] + gram[2 * ranks :])
    gram = gram[:, :ranks] + (gram[:, ranks : 2 * ranks] + gram[:, 2 * ranks :])
    return both[:ranks] + both[ranks:] + rest, gram


def paired_kernel(factor_ref, kept_ref, arrived_ref, out_ref, high_out, low_out, arrived, sems):
    rows, columns = kept_ref.shape
    ranks = factor_ref.shape[1]
    copies = []
    for c in range(columns // CHUNK):
        here = slice(c * CHUNK, (c + 1) * CHUNK)
        copies.append(pltpu.make_async_copy(arrived_ref.at[:, here], arrived.at[:, here], sems.at[c]))
        copies[-1].start()
    totals = no_totals(ranks, rows)
    for c, copy in enumerate(copies):
        here = slice(c * CHUNK, (c + 1) * CHUNK)
        copy.wait()
        high, low = halves(kept_ref[:, here] + arrived[:, here])
        high_out[:, here] = high
        low_out[:, here] = low
        totals = added_projection(totals, chunk_of(factor_ref, c), high, low)
    proj, gram = closed(totals)
    out_ref[:, :rows] = proj
    out_ref[:, rows:] = jnp.concatenate([gram, jnp.zeros((ranks, LANES - ranks), F32)], axis=1)


def half_projection(factor_ref, merged_ref):
    rows, columns = merged_ref.shape
    totals = no_totals(factor_ref.shape[1], rows)
    for c in range(columns // CHUNK):
        high, low = halves(merged_ref[:, c * CHUNK : (c + 1) * CHUNK])
        totals = added_projection(totals, chunk_of(factor_ref, c), high, low)
    return closed(totals)


def near_kernel(factor_ref, merged_ref, away_ref, out_ref, gram_ref, brought_ref, sem):
    copy = pltpu.make_async_copy(away_ref, brought_ref, sem)
    copy.start()
    out_ref[...], gram_ref[...] = half_projection(factor_ref, merged_ref)
    copy.wait()


def far_kernel(factor_ref, merged_ref, given_ref, given_gram_ref, out_ref, gram_ref):
    proj, gram = half_projection(factor_ref, merged_ref)
    out_ref[...] = given_ref[...] + proj
    gram_ref[...] = given_gram_ref[...] + gram


def three_rows(value):
    high, low = halves(value)
    return jnp.concatenate([high, high, low], axis=0)


def finish_kernel(
    kept_ref, away_ref, near_ref, far_ref, momentum_ref, weights_ref, proj_ref, summed_ref, inverse_ref,
    error_ref, new_momentum_ref, new_weights_ref, basis_ref, left, errors, momenta, stepped, sems,
):
    rows, columns = momentum_ref.shape
    count = columns // 2 // CHUNK
    inverse = inverse_ref[...]
    basis = dot(inverse, summed_ref[...], precision=HIGHEST)
    basis_ref[...] = basis
    left[:rows] = stacked_columns(dot(inverse, proj_ref[...], precision=HIGHEST))
    left[rows:] = stacked_columns(basis * 0.125)
    high, low = halves(inverse)
    turn = jnp.concatenate([high, low, high], axis=1)
    leaving = []
    for c in range(2 * count):
        here = slice(c * CHUNK, (c + 1) * CHUNK)
        own, place = c < count, c % count
        there = column(side_of(own), place, columns)
        factor_rows = three_rows(dot(turn, three_rows(chunk_of(near_ref if own else far_ref, place))))
        merged = (kept_ref if own else away_ref)[:, place * CHUNK : (place + 1) * CHUNK]
        errors[:, here] = merged - dot(left[:rows], factor_rows)
        update = dot(left[rows:], factor_rows)
        new_momentum = outer_beta * momentum_ref[:, there] + update
        momenta[:, here] = new_momentum
        step = outer_rate * (update + outer_beta * new_momentum)
        stepped[:, here] = (weights_ref[:, there].astype(F32) - step).astype(BF16)
        pairs = ((errors, error_ref.at[0]), (momenta, new_momentum_ref), (stepped, new_weights_ref))
        for i, (source, target) in enumerate(pairs):
            copy = pltpu.make_async_copy(source.at[:, here], target.at[:, there], sems.at[i, c])
            copy.start()
            leaving.append(copy)
    for copy in leaving:
        copy.wait()


def wide(rows):
    return pl.BlockSpec((rows, WIDE), lambda i: (0, i))


def whole(*shape):
    return pl.BlockSpec(shape, lambda i: (0,) * len(shape))


def blocks(ranks):
    return pl.BlockSpec((PER, ranks, LANES), lambda i: (i, 0, 0))


def call(kernel, columns, in_specs, outs, scratch=(), flops=0, traffic=0, limit=24):
    shapes = [jax.ShapeDtypeStruct(shape, kind) for shape, kind, _ in outs]
    specs = [spec for _, _, spec in outs]
    return pl.pallas_call(
        kernel,
        grid=(columns // WIDE,),
        in_specs=in_specs,
        out_shape=shapes,
        out_specs=specs,
        scratch_shapes=list(scratch),
        compiler_params=pltpu.CompilerParams(vmem_limit_bytes=limit * 2**20),
        cost_estimate=pl.CostEstimate(flops=flops, bytes_accessed=traffic, transcendentals=0),
    )


def around(axis, distance):
    size = lax.axis_size(axis)
    return [(i, (i + distance) % size) for i in range(size)]


def summed_directly(value, axis):
    size = lax.axis_size(axis)
    arrived = [lax.ppermute(value, axis, around(axis, d)) for d in range(1, size)]
    total = value
    for other in arrived:
        total = total + other
    return total


def to_everyone(piece, axes):
    size = lax.axis_size(axes)
    copies = jnp.broadcast_to(piece[None], (size, *piece.shape))
    return lax.all_to_all(copies, axes, 0, 0, tiled=True)


def over_chips(pieces):
    piece = lax.all_to_all(pieces, ("y", "x"), 0, 0, tiled=True).sum(axis=0)
    piece = to_everyone(piece, "z").sum(axis=0)
    return to_everyone(piece, ("y", "x"))


def spread(tile, column):
    return jnp.broadcast_to(tile[:, column : column + 1], tile.shape)


def inverse_kernel(gram_ref, anchor_ref, out_ref):
    ranks = out_ref.shape[0]
    gram = gram_ref[:, :ranks]
    row = lax.broadcasted_iota(jnp.int32, (ranks, ranks), 0)
    diagonal = row == lax.broadcasted_iota(jnp.int32, (ranks, ranks), 1)
    kept = jnp.where(diagonal, gram, 0.0)
    across = lax.rsqrt(jnp.sum(kept, axis=0, keepdims=True))
    down = lax.rsqrt(jnp.sum(kept, axis=1, keepdims=True))
    work = jnp.concatenate([gram * down * across, jnp.where(diagonal, across, 0.0)], axis=1)
    tiles = [work[8 * t : 8 * t + 8] for t in range(ranks // 8)]
    row = lax.broadcasted_iota(jnp.int32, (8, 2 * ranks), 0)
    out = []
    for j in range(0, ranks, 2):
        t, s = divmod(j, 8)
        left, right = spread(tiles[t], j), spread(tiles[t], j + 1)
        top, low = tiles[t][s : s + 1], tiles[t][s + 1 : s + 2]
        a, b, d = left[s : s + 1], left[s + 1 : s + 2], right[s + 1 : s + 2]
        det = a * d - b * b
        over = 1.0 / det
        rest = a * low - b * top
        first = (d * top - b * low) * over
        second = rest * over
        out.append(top * lax.rsqrt(a))
        out.append(rest * lax.rsqrt(a * det))
        for k in range(t, ranks // 8):
            if k > t:
                left, right = spread(tiles[k], j), spread(tiles[k], j + 1)
            elif s < 6:
                left = jnp.where(row > s + 1, left, 0.0)
                right = jnp.where(row > s + 1, right, 0.0)
            else:
                continue
            tiles[k] = tiles[k] - left * first - right * second
    out_ref[...] = jnp.concatenate(out, axis=0)[:, ranks:]


def inverse_factor(gram, anchor, block=0):
    ranks, width = gram.shape
    return pl.pallas_call(
        inverse_kernel,
        grid=(1,),
        in_specs=[
            pl.BlockSpec((ranks, min(width, LANES)), lambda i: (0, block)),
            pl.BlockSpec(memory_space=pl.ANY),
        ],
        out_specs=pl.BlockSpec((ranks, ranks), lambda i: (0, 0)),
        out_shape=jax.ShapeDtypeStruct((ranks, ranks), F32),
        compiler_params=pltpu.CompilerParams(vmem_limit_bytes=8 * 2**20),
        cost_estimate=pl.CostEstimate(flops=2 * 10**9, bytes_accessed=2**20, transcendentals=0),
    )(gram, anchor)


IN_VMEM = pl.BlockSpec(memory_space=pltpu.VMEM)
IN_HBM = pl.BlockSpec(memory_space=pltpu.HBM)


def in_hbm(array):
    return pltpu.with_memory_space_constraint(array, pltpu.HBM)


def flat_call(kernel, in_specs, out_shape, out_specs, scratch, flops, traffic):
    return pl.pallas_call(
        kernel,
        in_specs=in_specs,
        out_shape=out_shape,
        out_specs=out_specs,
        scratch_shapes=scratch,
        compiler_params=pltpu.CompilerParams(vmem_limit_bytes=24 * 2**20),
        cost_estimate=pl.CostEstimate(flops=flops, bytes_accessed=traffic, transcendentals=0),
    )


def merged_half(own, pseudo_grad, error_buffer, basis_t, anchor):
    _, rows, columns = pseudo_grad.shape
    ranks = basis_t.shape[0]
    half = columns // 2
    return flat_call(
        functools.partial(merge_kernel, own),
        [IN_HBM] * 3 + [pl.BlockSpec(memory_space=pl.ANY)],
        [pltpu.HBM((rows, half), F32), jax.ShapeDtypeStruct((half // LANES, ranks, LANES), F32)],
        [IN_HBM, IN_VMEM],
        [
            pltpu.VMEM((rows, half), F32),
            pltpu.VMEM((rows, half), F32),
            pltpu.VMEM((ranks, rows), F32),
            pltpu.SemaphoreType.DMA((3, half // CHUNK + 1)),
        ],
        6 * rows * half * ranks,
        12 * rows * half,
    )(in_hbm(pseudo_grad), in_hbm(error_buffer), in_hbm(basis_t), anchor)


def paired_product(factor, kept, arrived):
    _, ranks, _ = factor.shape
    rows, half = kept.shape
    share = jax.ShapeDtypeStruct((rows, half), BF16)
    return flat_call(
        paired_kernel,
        [IN_VMEM, IN_VMEM, IN_HBM],
        [jax.ShapeDtypeStruct((ranks, rows + LANES), F32), share, share],
        [IN_VMEM] * 3,
        [pltpu.VMEM((rows, half), F32), pltpu.SemaphoreType.DMA((half // CHUNK,))],
        6 * rows * half * ranks,
        12 * rows * half,
    )(factor, kept, in_hbm(arrived))


def near_product(factor, kept, away):
    _, ranks, _ = factor.shape
    rows, half = kept.shape
    return flat_call(
        near_kernel,
        [IN_VMEM, IN_VMEM, IN_HBM],
        [
            jax.ShapeDtypeStruct((ranks, rows), F32),
            jax.ShapeDtypeStruct((ranks, ranks), F32),
            jax.ShapeDtypeStruct((rows, half), F32),
        ],
        [IN_VMEM] * 3,
        [pltpu.SemaphoreType.DMA],
        6 * rows * half * ranks,
        8 * rows * half,
    )(factor, kept, in_hbm(away))


def far_product(factor, merged, proj_t, gram):
    _, ranks, _ = factor.shape
    rows, half = merged.shape
    return flat_call(
        far_kernel,
        [IN_VMEM] * 4,
        [jax.ShapeDtypeStruct((ranks, rows), F32), jax.ShapeDtypeStruct((ranks, ranks), F32)],
        [IN_VMEM] * 2,
        [],
        6 * rows * half * ranks,
        4 * rows * half,
    )(factor, merged, proj_t, gram)


def on_device(pseudo_grad, error_buffer, momentum, weights, warm_basis):
    _, rows, columns = pseudo_grad.shape
    ranks = warm_basis.shape[1]
    count = columns // LANES
    flops = 6 * rows * columns * ranks
    size = 4 * rows * columns
    short = whole(ranks, rows)
    square = whole(ranks, ranks)
    basis_t = warm_basis.T

    away, given = merged_half(False, pseudo_grad, error_buffer, basis_t, basis_t)
    kept, share = merged_half(True, pseudo_grad, error_buffer, basis_t, given)
    share = share + lax.ppermute(given, "core", SIBLING)
    share, leaving = lax.optimization_barrier((share, away))
    arrived = lax.ppermute(leaving, "core", SIBLING)
    proj_t, high_half, low_half = paired_product(over_chips(share), kept, arrived)
    paired = summed_directly(proj_t, "core")
    summed_t = summed_directly(paired[:, :rows], "y")
    inverse = inverse_factor(paired, paired, rows // LANES)
    (partial_blocks,) = call(
        partial_kernel,
        columns // 2,
        [wide(rows), wide(rows), short, square],
        [((count // 2, ranks, LANES), F32, blocks(ranks))],
        [pltpu.VMEM((ranks, rows), F32)],
        flops=flops // 2,
        traffic=size // 2,
    )(high_half, low_half, summed_t, inverse)
    near = over_chips(partial_blocks)
    far = lax.ppermute(near, "core", SIBLING)
    proj_t, gram, away = near_product(near, kept, away)
    proj_t, gram = far_product(far, away, proj_t, gram)
    paired = summed_directly(proj_t, "core")
    summed_t = summed_directly(paired, "y")
    inverse = inverse_factor(gram, paired)
    new_error, new_momentum, new_weights, basis_t = flat_call(
        finish_kernel,
        [IN_VMEM] * 9,
        [
            pltpu.HBM((1, rows, columns), F32),
            pltpu.HBM((rows, columns), F32),
            pltpu.HBM((rows, columns), BF16),
            jax.ShapeDtypeStruct((ranks, rows), F32),
        ],
        [IN_HBM] * 3 + [IN_VMEM],
        [
            pltpu.VMEM((2 * rows, 3 * ranks), BF16),
            pltpu.VMEM((rows, columns), F32),
            pltpu.VMEM((rows, columns), F32),
            pltpu.VMEM((rows, columns), BF16),
            pltpu.SemaphoreType.DMA((3, columns // CHUNK)),
        ],
        2 * flops,
        5 * size,
    )(kept, away, near, far, momentum, weights, proj_t, summed_t, inverse)
    return new_error, new_momentum, new_weights, basis_t.T


def solution(mesh):
    grid = Mesh(mesh.devices.reshape(4, 2, 4, 8), ("y", "core", "x", "z"))
    island, shard = ("y", "core"), ("x", "z")
    in_specs = (
        P(island, shard, None),
        P(island, shard, None),
        P(shard, None),
        P(shard, None),
        P(shard, None),
    )
    out_specs = (P(island, shard, None), P(shard, None), P(shard, None), P(shard, None))
    return jax.shard_map(
        on_device, mesh=grid, in_specs=in_specs, out_specs=out_specs, check_vma=False
    )
```

time: 139 us -> 132 us (0.950)
  blocking collectives: 70.9 us -> 83.5 us
  waiting for transfers between devices: 14.7 us -> 5.23 us
  Pallas kernels: 29.4 us -> 24.6 us
  starting transfers between devices: 20.8 us -> 17 us
    all_to_all x3 -> x4, blocking collectives: 41 us -> 53.9 us  [to_everyone(): return lax.all_to_all(copies, axes, 0, 0, tiled=True)]
    all_to_all x1 -> x0, waiting for transfers between devices: 8.99 us -> none  [to_everyone(): return lax.all_to_all(copies, axes, 0, 0, tiled=True)]
    pallas_call x5 -> x6, Pallas kernels: 22 us -> 17.2 us  [the longest x2 6.39 us: merged_half(): flat_call(functools.partial(merge_kernel, own), [IN_HBM] * 3 + [pl.BlockS...]
    all_to_all x1 -> x0, starting transfers between devices: 4.16 us -> none  [to_everyone(): return lax.all_to_all(copies, axes, 0, 0, tiled=True)]
    ppermute x3, waiting for transfers between devices: 2.9 us -> 0.01 us  [the longest x1 0.01 us: on_device(): share = share + lax.ppermute(given, 'core', SIBLING)]
    ppermute x8, waiting for transfers between devices: 2.8 us -> 5.22 us  [summed_directly(): lax.ppermute(value, axis, around(axis, d))]
  transfers between devices with their start and end apart: 12 -> 11, of which waited for: 6 -> 5; matrix products, arithmetic and copies ran while one was open for 1% -> 0% of each run, Pallas kernels for 8% -> 9%
where the time goes in v2:
time: 132 us
  blocking collectives  83.5 us (63%)
  Pallas kernels  24.6 us (19%)
  starting transfers between devices  17 us (13%)
  waiting for transfers between devices  5.23 us (4%)
    all_to_all x4, blocking collectives, to_everyone(): return lax.all_to_all(copies, axes, 0, 0, tiled=True)  53.9 us
    all_to_all x2, blocking collectives, over_chips(): piece = lax.all_to_all(pieces, ('y', 'x'), 0, 0, tiled=True).sum(axis=0)  29.6 us
    ppermute x8, starting transfers between devices, summed_directly(): lax.ppermute(value, axis, around(axis, d))  8.69 us
    pallas_call x2, Pallas kernels, inverse_factor(): pl.pallas_call(inverse_kernel, grid=(1,), in_specs=[pl.BlockSpec((ranks,...  6.46 us
    pallas_call x2, Pallas kernels, merged_half(): flat_call(functools.partial(merge_kernel, own), [IN_HBM] * 3 + [pl.BlockS...  6.39 us
    pallas_call x1, Pallas kernels, on_device(): flat_call(finish_kernel, [IN_VMEM] * 9, [pltpu.HBM((1, rows, columns), F3...  5.47 us
    ppermute x8, waiting for transfers between devices, summed_directly(): lax.ppermute(value, axis, around(axis, d))  5.22 us
    ppermute x1, starting transfers between devices, on_device(): far = lax.ppermute(near, 'core', SIBLING)  4.85 us
  transfers between devices with their start and end apart: 11, of which 5 were waited for; matrix products, arithmetic and copies ran while one was open for 0% of the time, Pallas kernels for 9%

profile of v2, /device:TPU:1, one launch (start us, length us, event | category | flops | bytes accessed | tf_op | source)
XLA Modules:
  0.0 131.7 jit_solution(12975682904504254726)
XLA Ops:
  0.6 3.2 %shard_map.84 = (f32[256,2048]{1,0:T(8,128)}, f32[16,64,128]{2,1,0:T(8,128)S(1)}) custom-call(f32[1,256,4096]{2,1,0:T(8,128)} %grad_ref.3, f32[1,256,4096]{2,1,0:T(8,128)} %error_ref.3, f32[64,256]{1,0:T(8,128)} %bitcast.2, f32[64,256]{1,0:T(8,128)} %bitcast.3), custom_call_target="tpu_custom_call" | custom-call | flops 201326592 | bytes 6291456 | tf_op jit(solution)/shard_map/pallas_call | solution.py:355
  3.8 3.3 %collective-permute-start = (f32[16,64,128]{2,1,0:T(8,128)S(1)}, f32[16,64,128]{2,1,0:T(8,128)S(1)}, u32[]{:S(2)}, u32[]{:S(2)}) collective-permute-start(f32[16,64,128]{2,1,0:T(8,128)S(1)} %get-tuple-element.22.anchor_ref), channel_id=1, source_target_pairs={{0,32},{32,0},{1,33},{33,1},{2,34},{34,2},{3,35},{35,3},{4,36},{36... | collective-permute-start | bytes 1572872 | tf_op jit(solution)/shard_map/ppermute | solution.py:430
  7.2 3.2 %shard_map.85 = (f32[256,2048]{1,0:T(8,128)}, f32[16,64,128]{2,1,0:T(8,128)S(1)}) custom-call(f32[1,256,4096]{2,1,0:T(8,128)} %grad_ref.3, f32[1,256,4096]{2,1,0:T(8,128)} %error_ref.3, f32[64,256]{1,0:T(8,128)} %bitcast.4, f32[16,64,128]{2,1,0:T(8,128)S(1)} %get-tuple-element.22.anchor_ref), custom_call_target="tpu_custom_call" | custom-call | flops 201326592 | bytes 6291456 | tf_op jit(solution)/shard_map/pallas_call | solution.py:355
  10.4 0.1 add.27
  10.5 0.1 collective-permute-start.1
  10.6 15.5 %all_to_all.30 = f32[16,64,128]{2,1,0:T(8,128)S(1)} all-to-all(f32[16,64,128]{2,1,0:T(8,128)S(1)} %add.27), channel_id=1, replica_groups=mesh['y'=4,'core'=2,'x'=4,'z'=8] {'y','x'}, dimensions={0} | all-to-all | bytes 1048576 | tf_op jit(solution)/shard_map/all_to_all | solution.py:270
  26.2 17.4 %all_to_all.31 = f32[8,64,128]{2,1,0:T(8,128)S(1)} all-to-all(f32[8,64,128]{2,1,0:T(8,128)S(1)} %broadcast_in_dim.8), channel_id=1, replica_groups=mesh['y'=4,'core'=2,'x'=4,'z'=8] {'z'}, dimensions={0} | all-to-all | bytes 524288 | tf_op jit(solution)/shard_map/all_to_all | solution.py:266
  43.6 12.8 %all_to_all.32.factor_ref = f32[16,64,128]{2,1,0:T(8,128)S(1)} all-to-all(f32[16,64,128]{2,1,0:T(8,128)S(1)} %broadcast_in_dim.9), channel_id=1, replica_groups=mesh['y'=4,'core'=2,'x'=4,'z'=8] {'y','x'}, dimensions={0} | all-to-all | bytes 1048576 | tf_op jit(solution)/shard_map/all_to_all | solution.py:266
  56.4 2.6 %shard_map.86 = (f32[64,384]{1,0:T(8,128)S(1)}, bf16[256,2048]{1,0:T(8,128)(2,1)S(1)}, bf16[256,2048]{1,0:T(8,128)(2,1)S(1)}) custom-call(f32[16,64,128]{2,1,0:T(8,128)S(1)} %all_to_all.32.factor_ref, f32[256,2048]{1,0:T(8,128)S(1)} %copy-done, f32[256,2048]{1,0:T(8,128)} %collective-permute-done.1.arrived_ref), custom_call_target="tpu_custom_call" | custom-call | flops 201326592 | bytes 6291456 | tf_op jit(solution)/shard_map/pallas_call | solution.py:375
  59.0 4.5 %collective-permute-start.2 = (f32[64,384]{1,0:T(8,128)S(1)}, f32[64,384]{1,0:T(8,128)S(1)}, u32[]{:S(2)}, u32[]{:S(2)}) collective-permute-start(f32[64,384]{1,0:T(8,128)S(1)} %get-tuple-element.30), channel_id=1, source_target_pairs={{0,32},{32,0},{1,33},{33,1},{2,34},{34,2},{3,35},{35,3},{4,36},{36... | collective-permute-start | bytes 294920 | tf_op jit(solution)/shard_map/ppermute | solution.py:256
  63.5 0.9 collective-permute-done.2
  64.5 0.7 collective-permute-start.4
  65.1 1.3 collective-permute-start.5
  66.4 0.2 collective-permute-start.3
  66.6 3.2 %shard_map.87.inverse_ref = f32[64,64]{1,0:T(8,128)S(1)} custom-call(f32[64,384]{1,0:T(8,128)S(1)} %add.28.gram_ref.anchor_ref, f32[64,384]{1,0:T(8,128)S(1)} %add.28.gram_ref.anchor_ref), custom_call_target="tpu_custom_call" | custom-call | flops 2000000000 | bytes 1048576 | tf_op jit(solution)/shard_map/pallas_call | solution.py:317
  69.8 0.9 collective-permute-done.3
  70.8 1.0 shard_map.88
  71.8 14.1 %all_to_all.33 = f32[16,64,128]{2,1,0:T(8,128)S(1)} all-to-all(f32[16,64,128]{2,1,0:T(8,128)S(1)} %shard_map.88), channel_id=1, replica_groups=mesh['y'=4,'core'=2,'x'=4,'z'=8] {'y','x'}, dimensions={0} | all-to-all | bytes 1048576 | tf_op jit(solution)/shard_map/all_to_all | solution.py:270
  85.9 11.8 %all_to_all.34 = f32[8,64,128]{2,1,0:T(8,128)S(1)} all-to-all(f32[8,64,128]{2,1,0:T(8,128)S(1)} %broadcast_in_dim.10), channel_id=1, replica_groups=mesh['y'=4,'core'=2,'x'=4,'z'=8] {'z'}, dimensions={0} | all-to-all | bytes 524288 | tf_op jit(solution)/shard_map/all_to_all | solution.py:266
  97.8 11.9 %all_to_all.35.factor_ref.near_ref = f32[16,64,128]{2,1,0:T(8,128)S(1)} all-to-all(f32[16,64,128]{2,1,0:T(8,128)S(1)} %broadcast_in_dim.11), channel_id=1, replica_groups=mesh['y'=4,'core'=2,'x'=4,'z'=8] {'y','x'}, dimensions={0} | all-to-all | bytes 1048576 | tf_op jit(solution)/shard_map/all_to_all | solution.py:266
  109.7 4.9 %collective-permute-start.6 = (f32[16,64,128]{2,1,0:T(8,128)S(1)}, f32[16,64,128]{2,1,0:T(8,128)S(1)}, u32[]{:S(2)}, u32[]{:S(2)}) collective-permute-start(f32[16,64,128]{2,1,0:T(8,128)S(1)} %all_to_all.35.factor_ref.near_ref), channel_id=1, source_target_pairs={{0,32},{32,0},{1,33},{33,1},{2,34},{34,2},{3,35},{35,3},{4,36},{36... | collective-permute-start | bytes 1572872 | tf_op jit(solution)/shard_map/ppermute | solution.py:447
  114.6 1.6 %shard_map.89 = (f32[64,256]{1,0:T(8,128)S(1)}, f32[64,64]{1,0:T(8,128)S(1)}, f32[256,2048]{1,0:T(8,128)S(1)}) custom-call(f32[16,64,128]{2,1,0:T(8,128)S(1)} %all_to_all.35.factor_ref.near_ref, f32[256,2048]{1,0:T(8,128)S(1)} %copy-done, f32[256,2048]{1,0:T(8,128)} %get-tuple-element.27.away_ref), custom_call_target="tpu_custom_call" | custom-call | flops 201326592 | bytes 4194304 | tf_op jit(solution)/shard_map/pallas_call | solution.py:389
  116.2 1.1 shard_map.90
  117.3 0.4 collective-permute-start.7
  117.7 1.0 collective-permute-done.7
  118.7 0.8 collective-permute-start.10
  119.5 0.7 collective-permute-start.9
  120.3 0.2 collective-permute-start.8
  120.4 3.2 %shard_map.91.inverse_ref = f32[64,64]{1,0:T(8,128)S(1)} custom-call(f32[64,64]{1,0:T(8,128)S(1)} %get-tuple-element.35.gram_ref, f32[64,256]{1,0:T(8,128)S(1)} %add.32.anchor_ref), custom_call_target="tpu_custom_call" | custom-call | flops 2000000000 | bytes 1048576 | tf_op jit(solution)/shard_map/pallas_call | solution.py:317
  123.7 0.5 collective-permute-done.9
  124.2 1.8 %collective-permute-done.8 = f32[64,256]{1,0:T(8,128)S(1)} collective-permute-done((f32[64,256]{1,0:T(8,128)S(1)}, f32[64,256]{1,0:T(8,128)S(1)}, u32[]{:S(2)}, u32[]{:S(2)}) %collective-permute-start.8) | collective-permute-done | bytes 65568 | tf_op jit(solution)/shard_map/ppermute | solution.py:256
  126.1 5.5 %shard_map.92 = (f32[1,256,4096]{2,1,0:T(8,128)}, f32[256,4096]{1,0:T(8,128)}, bf16[256,4096]{1,0:T(8,128)(2,1)}, f32[64,256]{1,0:T(8,128)}) custom-call(f32[256,2048]{1,0:T(8,128)S(1)} %copy-done, f32[256,2048]{1,0:T(8,128)S(1)} %get-tuple-element.31.merged_ref.away_ref, f32[16,64,128]{2,1,0:T(8,128)S(1)} %all_to_all.35.factor_ref.near_ref, ...), custom_call_target="tpu_custom_call" | custom-call | flops 805306368 | bytes 20971520 | tf_op jit(solution)/shard_map/pallas_call | solution.py:453
  (25 shorter events, 0.3 us)
Async XLA Ops:
  3.8 6.5 %collective-permute-start = (f32[16,64,128]{2,1,0:T(8,128)S(1)}, f32[16,64,128]{2,1,0:T(8,128)S(1)}, u32[]{:S(2)}, u32[]{:S(2)}) collective-permute-start(f32[16,64,128]{2,1,0:T(8,128)S(1)} %get-tuple-element.22.anchor_ref), channel_id=1, source_target_pairs={{0,32},{32,0},{1,33},{33,1},{2,34},{34,2},{3,35},{35,3},{4,36},{36... | collective-permute-start | bytes 1572872 | tf_op jit(solution)/shard_map/ppermute | solution.py:430
  10.4 46.0 %copy-start = (f32[256,2048]{1,0:T(8,128)S(1)}, f32[256,2048]{1,0:T(8,128)}, u32[]{:S(2)}) copy-start(f32[256,2048]{1,0:T(8,128)} %get-tuple-element.23.kept_ref.merged_ref) | copy-start | bytes 6291460
  10.5 45.9 %collective-permute-start.1 = (f32[256,2048]{1,0:T(8,128)}, f32[256,2048]{1,0:T(8,128)}, u32[]{:S(2)}, u32[]{:S(2)}) collective-permute-start(f32[256,2048]{1,0:T(8,128)} %get-tuple-element.27.away_ref), channel_id=1, source_target_pairs={{0,32},{32,0},{1,33},{33,1},{2,34},{34,2},{3,35},{35,3},{4,36},{36... | collective-permute-start | bytes 6291464 | tf_op jit(solution)/shard_map/ppermute | solution.py:432
  59.0 5.4 %collective-permute-start.2 = (f32[64,384]{1,0:T(8,128)S(1)}, f32[64,384]{1,0:T(8,128)S(1)}, u32[]{:S(2)}, u32[]{:S(2)}) collective-permute-start(f32[64,384]{1,0:T(8,128)S(1)} %get-tuple-element.30), channel_id=1, source_target_pairs={{0,32},{32,0},{1,33},{33,1},{2,34},{34,2},{3,35},{35,3},{4,36},{36... | collective-permute-start | bytes 294920 | tf_op jit(solution)/shard_map/ppermute | solution.py:256
  64.5 5.4 %collective-permute-start.4 = (f32[64,256]{1,0:T(8,128)S(1)}, f32[64,256]{1,0:T(8,128)S(1)}, u32[]{:S(2)}, u32[]{:S(2)}) collective-permute-start(f32[64,256]{1,0:T(8,128)S(1)} %slice.4), channel_id=1, source_target_pairs={{0,128},{64,192},{128,0},{192,64},{1,129},{65,193},{129,1},{193,65... | collective-permute-start | bytes 196616 | tf_op jit(solution)/shard_map/ppermute | solution.py:256
  65.1 4.7 %collective-permute-start.5 = (f32[64,256]{1,0:T(8,128)S(1)}, f32[64,256]{1,0:T(8,128)S(1)}, u32[]{:S(2)}, u32[]{:S(2)}) collective-permute-start(f32[64,256]{1,0:T(8,128)S(1)} %slice.4), channel_id=1, source_target_pairs={{0,192},{64,0},{128,64},{192,128},{1,193},{65,1},{129,65},{193,129... | collective-permute-start | bytes 196616 | tf_op jit(solution)/shard_map/ppermute | solution.py:256
  66.4 4.4 %collective-permute-start.3 = (f32[64,256]{1,0:T(8,128)S(1)}, f32[64,256]{1,0:T(8,128)S(1)}, u32[]{:S(2)}, u32[]{:S(2)}) collective-permute-start(f32[64,256]{1,0:T(8,128)S(1)} %slice.4), channel_id=1, source_target_pairs={{0,64},{64,128},{128,192},{192,0},{1,65},{65,129},{129,193},{193,1... | collective-permute-start | bytes 196616 | tf_op jit(solution)/shard_map/ppermute | solution.py:256
  109.7 6.5 %collective-permute-start.6 = (f32[16,64,128]{2,1,0:T(8,128)S(1)}, f32[16,64,128]{2,1,0:T(8,128)S(1)}, u32[]{:S(2)}, u32[]{:S(2)}) collective-permute-start(f32[16,64,128]{2,1,0:T(8,128)S(1)} %all_to_all.35.factor_ref.near_ref), channel_id=1, source_target_pairs={{0,32},{32,0},{1,33},{33,1},{2,34},{34,2},{3,35},{35,3},{4,36},{36... | collective-permute-start | bytes 1572872 | tf_op jit(solution)/shard_map/ppermute | solution.py:447
  117.3 1.3 %collective-permute-start.7 = (f32[64,256]{1,0:T(8,128)S(1)}, f32[64,256]{1,0:T(8,128)S(1)}, u32[]{:S(2)}, u32[]{:S(2)}) collective-permute-start(f32[64,256]{1,0:T(8,128)S(1)} %get-tuple-element.34.proj_ref), channel_id=1, source_target_pairs={{0,32},{32,0},{1,33},{33,1},{2,34},{34,2},{3,35},{35,3},{4,36},{36... | collective-permute-start | bytes 196616 | tf_op jit(solution)/shard_map/ppermute | solution.py:256
  118.7 5.0 %collective-permute-start.10 = (f32[64,256]{1,0:T(8,128)S(1)}, f32[64,256]{1,0:T(8,128)S(1)}, u32[]{:S(2)}, u32[]{:S(2)}) collective-permute-start(f32[64,256]{1,0:T(8,128)S(1)} %add.32.anchor_ref), channel_id=1, source_target_pairs={{0,192},{64,0},{128,64},{192,128},{1,193},{65,1},{129,65},{193,129... | collective-permute-start | bytes 196616 | tf_op jit(solution)/shard_map/ppermute | solution.py:256
  119.5 4.6 %collective-permute-start.9 = (f32[64,256]{1,0:T(8,128)S(1)}, f32[64,256]{1,0:T(8,128)S(1)}, u32[]{:S(2)}, u32[]{:S(2)}) collective-permute-start(f32[64,256]{1,0:T(8,128)S(1)} %add.32.anchor_ref), channel_id=1, source_target_pairs={{0,128},{64,192},{128,0},{192,64},{1,129},{65,193},{129,1},{193,65... | collective-permute-start | bytes 196616 | tf_op jit(solution)/shard_map/ppermute | solution.py:256
  120.3 5.8 %collective-permute-start.8 = (f32[64,256]{1,0:T(8,128)S(1)}, f32[64,256]{1,0:T(8,128)S(1)}, u32[]{:S(2)}, u32[]{:S(2)}) collective-permute-start(f32[64,256]{1,0:T(8,128)S(1)} %add.32.anchor_ref), channel_id=1, source_target_pairs={{0,64},{64,128},{128,192},{192,0},{1,65},{65,129},{129,193},{193,1... | collective-permute-start | bytes 196616 | tf_op jit(solution)/shard_map/ppermute | solution.py:256
  120.4 5.6 %copy-start.1 = (f32[256,4096]{1,0:T(8,128)S(1)}, f32[256,4096]{1,0:T(8,128)}, u32[]{:S(2)}) copy-start(f32[256,4096]{1,0:T(8,128)} %momentum_ref.1) | copy-start | bytes 12582916
  120.4 5.6 %copy-start.2 = (bf16[256,4096]{1,0:T(8,128)(2,1)S(1)}, bf16[256,4096]{1,0:T(8,128)(2,1)}, u32[]{:S(2)}) copy-start(bf16[256,4096]{1,0:T(8,128)(2,1)} %weights_ref.1) | copy-start | bytes 6291460

commit v3 on v2

--- a/solution.py
+++ b/solution.py
@@ -85,10 +85,13 @@
         for copy in pair:
             copy.wait()
         merged = grads[:, here] + errors[:, here]
-        grads[:, here] = merged
-        copy = pltpu.make_async_copy(grads.at[:, here], merged_ref.at[:, here], sems.at[2, c])
-        copy.start()
-        leaving.append(copy)
+        if own:
+            merged_ref[:, here] = merged
+        else:
+            grads[:, here] = merged
+            copy = pltpu.make_async_copy(grads.at[:, here], merged_ref.at[:, here], sems.at[2, c])
+            copy.start()
+            leaving.append(copy)
         partial = rank_product(basis[...], *halves(merged))
         for j in range(CHUNK // LANES):
             partial_ref[c * (CHUNK // LANES) + j] = partial[:, j * LANES : (j + 1) * LANES]
@@ -352,11 +355,12 @@
     _, rows, columns = pseudo_grad.shape
     ranks = basis_t.shape[0]
     half = columns // 2
+    merged = jax.ShapeDtypeStruct((rows, half), F32) if own else pltpu.HBM((rows, half), F32)
     return flat_call(
         functools.partial(merge_kernel, own),
         [IN_HBM] * 3 + [pl.BlockSpec(memory_space=pl.ANY)],
-        [pltpu.HBM((rows, half), F32), jax.ShapeDtypeStruct((half // LANES, ranks, LANES), F32)],
-        [IN_HBM, IN_VMEM],
+        [merged, jax.ShapeDtypeStruct((half // LANES, ranks, LANES), F32)],
+        [IN_VMEM if own else IN_HBM, IN_VMEM],
         [
             pltpu.VMEM((rows, half), F32),
             pltpu.VMEM((rows, half), F32),

time: 132 us -> 131 us (level)
  transfers between devices with their start and end apart: 11 -> 11, of which waited for: 5 -> 5; matrix products, arithmetic and copies ran while one was open for 0% -> 0% of each run, Pallas kernels for 9% -> 8%
where the time goes in v3:
time: 131 us
  blocking collectives  83.4 us (64%)
  Pallas kernels  24 us (18%)
  starting transfers between devices  17 us (13%)
  waiting for transfers between devices  5.23 us (4%)
    all_to_all x4, blocking collectives, to_everyone(): return lax.all_to_all(copies, axes, 0, 0, tiled=True)  53.9 us
    all_to_all x2, blocking collectives, over_chips(): piece = lax.all_to_all(pieces, ('y', 'x'), 0, 0, tiled=True).sum(axis=0)  29.5 us
    ppermute x8, starting transfers between devices, summed_directly(): lax.ppermute(value, axis, around(axis, d))  8.69 us
    pallas_call x2, Pallas kernels, inverse_factor(): pl.pallas_call(inverse_kernel, grid=(1,), in_specs=[pl.BlockSpec((ranks,...  6.46 us
    pallas_call x2, Pallas kernels, merged_half(): flat_call(functools.partial(merge_kernel, own), [IN_HBM] * 3 + [pl.BlockS...  5.79 us
    pallas_call x1, Pallas kernels, on_device(): flat_call(finish_kernel, [IN_VMEM] * 9, [pltpu.HBM((1, rows, columns), F3...  5.47 us
    ppermute x8, waiting for transfers between devices, summed_directly(): lax.ppermute(value, axis, around(axis, d))  5.22 us
    ppermute x1, starting transfers between devices, on_device(): far = lax.ppermute(near, 'core', SIBLING)  4.85 us
  transfers between devices with their start and end apart: 11, of which 5 were waited for; matrix products, arithmetic and copies ran while one was open for 0% of the time, Pallas kernels for 8%

profile of v3, /device:TPU:1, one launch (start us, length us, event | category | flops | bytes accessed | tf_op | source)
XLA Modules:
  0.0 131.0 jit_solution(13052881112010982833)
XLA Ops:
  0.6 3.2 %shard_map.84 = (f32[256,2048]{1,0:T(8,128)}, f32[16,64,128]{2,1,0:T(8,128)S(1)}) custom-call(f32[1,256,4096]{2,1,0:T(8,128)} %grad_ref.3, f32[1,256,4096]{2,1,0:T(8,128)} %error_ref.3, f32[64,256]{1,0:T(8,128)} %bitcast.2, f32[64,256]{1,0:T(8,128)} %bitcast.3), custom_call_target="tpu_custom_call" | custom-call | flops 201326592 | bytes 6291456 | tf_op jit(solution)/shard_map/pallas_call | solution.py:359
  3.8 3.3 %collective-permute-start = (f32[16,64,128]{2,1,0:T(8,128)S(1)}, f32[16,64,128]{2,1,0:T(8,128)S(1)}, u32[]{:S(2)}, u32[]{:S(2)}) collective-permute-start(f32[16,64,128]{2,1,0:T(8,128)S(1)} %get-tuple-element.22.anchor_ref), channel_id=1, source_target_pairs={{0,32},{32,0},{1,33},{33,1},{2,34},{34,2},{3,35},{35,3},{4,36},{36... | collective-permute-start | bytes 1572872 | tf_op jit(solution)/shard_map/ppermute | solution.py:434
  7.2 2.6 %shard_map.85 = (f32[256,2048]{1,0:T(8,128)S(1)}, f32[16,64,128]{2,1,0:T(8,128)S(1)}) custom-call(f32[1,256,4096]{2,1,0:T(8,128)} %grad_ref.3, f32[1,256,4096]{2,1,0:T(8,128)} %error_ref.3, f32[64,256]{1,0:T(8,128)} %bitcast.4, f32[16,64,128]{2,1,0:T(8,128)S(1)} %get-tuple-element.22.anchor_ref), custom_call_target="tpu_custom_call" | custom-call | flops 201326592 | bytes 6291456 | tf_op jit(solution)/shard_map/pallas_call | solution.py:359
  9.8 0.1 add.27
  9.8 0.1 collective-permute-start.1
  9.9 15.4 %all_to_all.30 = f32[16,64,128]{2,1,0:T(8,128)S(1)} all-to-all(f32[16,64,128]{2,1,0:T(8,128)S(1)} %add.27), channel_id=1, replica_groups=mesh['y'=4,'core'=2,'x'=4,'z'=8] {'y','x'}, dimensions={0} | all-to-all | bytes 1048576 | tf_op jit(solution)/shard_map/all_to_all | solution.py:273
  25.4 17.4 %all_to_all.31 = f32[8,64,128]{2,1,0:T(8,128)S(1)} all-to-all(f32[8,64,128]{2,1,0:T(8,128)S(1)} %broadcast_in_dim.8), channel_id=1, replica_groups=mesh['y'=4,'core'=2,'x'=4,'z'=8] {'z'}, dimensions={0} | all-to-all | bytes 524288 | tf_op jit(solution)/shard_map/all_to_all | solution.py:269
  42.9 12.8 %all_to_all.32.factor_ref = f32[16,64,128]{2,1,0:T(8,128)S(1)} all-to-all(f32[16,64,128]{2,1,0:T(8,128)S(1)} %broadcast_in_dim.9), channel_id=1, replica_groups=mesh['y'=4,'core'=2,'x'=4,'z'=8] {'y','x'}, dimensions={0} | all-to-all | bytes 1048576 | tf_op jit(solution)/shard_map/all_to_all | solution.py:269
  55.7 2.6 %shard_map.86 = (f32[64,384]{1,0:T(8,128)S(1)}, bf16[256,2048]{1,0:T(8,128)(2,1)S(1)}, bf16[256,2048]{1,0:T(8,128)(2,1)S(1)}) custom-call(f32[16,64,128]{2,1,0:T(8,128)S(1)} %all_to_all.32.factor_ref, f32[256,2048]{1,0:T(8,128)S(1)} %get-tuple-element.23.kept_ref.merged_ref, f32[256,2048]{1,0:T(8,128)} %collective-permute-done.1.arrived_ref), custom_call_target="tpu_custom_call" | custom-call | flops 201326592 | bytes 6291456 | tf_op jit(solution)/shard_map/pallas_call | solution.py:379
  58.3 4.5 %collective-permute-start.2 = (f32[64,384]{1,0:T(8,128)S(1)}, f32[64,384]{1,0:T(8,128)S(1)}, u32[]{:S(2)}, u32[]{:S(2)}) collective-permute-start(f32[64,384]{1,0:T(8,128)S(1)} %get-tuple-element.30), channel_id=1, source_target_pairs={{0,32},{32,0},{1,33},{33,1},{2,34},{34,2},{3,35},{35,3},{4,36},{36... | collective-permute-start | bytes 294920 | tf_op jit(solution)/shard_map/ppermute | solution.py:259
  62.8 0.9 collective-permute-done.2
  63.7 0.7 collective-permute-start.4
  64.4 1.3 collective-permute-start.5
  65.7 0.2 collective-permute-start.3
  65.9 3.2 %shard_map.87.inverse_ref = f32[64,64]{1,0:T(8,128)S(1)} custom-call(f32[64,384]{1,0:T(8,128)S(1)} %add.28.gram_ref.anchor_ref, f32[64,384]{1,0:T(8,128)S(1)} %add.28.gram_ref.anchor_ref), custom_call_target="tpu_custom_call" | custom-call | flops 2000000000 | bytes 1048576 | tf_op jit(solution)/shard_map/pallas_call | solution.py:320
  69.1 0.9 collective-permute-done.3
  70.1 1.0 shard_map.88
  71.0 14.1 %all_to_all.33 = f32[16,64,128]{2,1,0:T(8,128)S(1)} all-to-all(f32[16,64,128]{2,1,0:T(8,128)S(1)} %shard_map.88), channel_id=1, replica_groups=mesh['y'=4,'core'=2,'x'=4,'z'=8] {'y','x'}, dimensions={0} | all-to-all | bytes 1048576 | tf_op jit(solution)/shard_map/all_to_all | solution.py:273
  85.2 11.8 %all_to_all.34 = f32[8,64,128]{2,1,0:T(8,128)S(1)} all-to-all(f32[8,64,128]{2,1,0:T(8,128)S(1)} %broadcast_in_dim.10), channel_id=1, replica_groups=mesh['y'=4,'core'=2,'x'=4,'z'=8] {'z'}, dimensions={0} | all-to-all | bytes 524288 | tf_op jit(solution)/shard_map/all_to_all | solution.py:269
  97.1 11.9 %all_to_all.35.factor_ref.near_ref = f32[16,64,128]{2,1,0:T(8,128)S(1)} all-to-all(f32[16,64,128]{2,1,0:T(8,128)S(1)} %broadcast_in_dim.11), channel_id=1, replica_groups=mesh['y'=4,'core'=2,'x'=4,'z'=8] {'y','x'}, dimensions={0} | all-to-all | bytes 1048576 | tf_op jit(solution)/shard_map/all_to_all | solution.py:269
  109.0 4.9 %collective-permute-start.6 = (f32[16,64,128]{2,1,0:T(8,128)S(1)}, f32[16,64,128]{2,1,0:T(8,128)S(1)}, u32[]{:S(2)}, u32[]{:S(2)}) collective-permute-start(f32[16,64,128]{2,1,0:T(8,128)S(1)} %all_to_all.35.factor_ref.near_ref), channel_id=1, source_target_pairs={{0,32},{32,0},{1,33},{33,1},{2,34},{34,2},{3,35},{35,3},{4,36},{36... | collective-permute-start | bytes 1572872 | tf_op jit(solution)/shard_map/ppermute | solution.py:451
  113.9 1.6 %shard_map.89 = (f32[64,256]{1,0:T(8,128)S(1)}, f32[64,64]{1,0:T(8,128)S(1)}, f32[256,2048]{1,0:T(8,128)S(1)}) custom-call(f32[16,64,128]{2,1,0:T(8,128)S(1)} %all_to_all.35.factor_ref.near_ref, f32[256,2048]{1,0:T(8,128)S(1)} %get-tuple-element.23.kept_ref.merged_ref, f32[256,2048]{1,0:T(8,128)} %get-tuple-element.27.away_ref), custom_call_target="tpu_custom_call" | custom-call | flops 201326592 | bytes 4194304 | tf_op jit(solution)/shard_map/pallas_call | solution.py:393
  115.5 1.1 shard_map.90
  116.6 0.4 collective-permute-start.7
  117.0 1.0 collective-permute-done.7
  118.0 0.8 collective-permute-start.10
  118.8 0.7 collective-permute-start.9
  119.5 0.2 collective-permute-start.8
  119.7 3.2 %shard_map.91.inverse_ref = f32[64,64]{1,0:T(8,128)S(1)} custom-call(f32[64,64]{1,0:T(8,128)S(1)} %get-tuple-element.35.gram_ref, f32[64,256]{1,0:T(8,128)S(1)} %add.32.anchor_ref), custom_call_target="tpu_custom_call" | custom-call | flops 2000000000 | bytes 1048576 | tf_op jit(solution)/shard_map/pallas_call | solution.py:320
  122.9 0.5 collective-permute-done.9
  123.4 1.8 %collective-permute-done.8 = f32[64,256]{1,0:T(8,128)S(1)} collective-permute-done((f32[64,256]{1,0:T(8,128)S(1)}, f32[64,256]{1,0:T(8,128)S(1)}, u32[]{:S(2)}, u32[]{:S(2)}) %collective-permute-start.8) | collective-permute-done | bytes 65568 | tf_op jit(solution)/shard_map/ppermute | solution.py:259
  125.3 5.5 %shard_map.92 = (f32[1,256,4096]{2,1,0:T(8,128)}, f32[256,4096]{1,0:T(8,128)}, bf16[256,4096]{1,0:T(8,128)(2,1)}, f32[64,256]{1,0:T(8,128)}) custom-call(f32[256,2048]{1,0:T(8,128)S(1)} %get-tuple-element.23.kept_ref.merged_ref, f32[256,2048]{1,0:T(8,128)S(1)} %get-tuple-element.31.merged_ref.away_ref, f32[16,64,128]{2,1,0:T(8,128)S(1)} %all_to_all.35.factor_ref.near_ref, ...), custom_call_target="tpu_custom_call" | custom-call | flops 805306368 | bytes 20971520 | tf_op jit(solution)/shard_map/pallas_call | solution.py:457
  (23 shorter events, 0.3 us)
Async XLA Ops:
  3.8 5.9 %collective-permute-start = (f32[16,64,128]{2,1,0:T(8,128)S(1)}, f32[16,64,128]{2,1,0:T(8,128)S(1)}, u32[]{:S(2)}, u32[]{:S(2)}) collective-permute-start(f32[16,64,128]{2,1,0:T(8,128)S(1)} %get-tuple-element.22.anchor_ref), channel_id=1, source_target_pairs={{0,32},{32,0},{1,33},{33,1},{2,34},{34,2},{3,35},{35,3},{4,36},{36... | collective-permute-start | bytes 1572872 | tf_op jit(solution)/shard_map/ppermute | solution.py:434
  9.8 45.8 %collective-permute-start.1 = (f32[256,2048]{1,0:T(8,128)}, f32[256,2048]{1,0:T(8,128)}, u32[]{:S(2)}, u32[]{:S(2)}) collective-permute-start(f32[256,2048]{1,0:T(8,128)} %get-tuple-element.27.away_ref), channel_id=1, source_target_pairs={{0,32},{32,0},{1,33},{33,1},{2,34},{34,2},{3,35},{35,3},{4,36},{36... | collective-permute-start | bytes 6291464 | tf_op jit(solution)/shard_map/ppermute | solution.py:436
  58.3 5.4 %collective-permute-start.2 = (f32[64,384]{1,0:T(8,128)S(1)}, f32[64,384]{1,0:T(8,128)S(1)}, u32[]{:S(2)}, u32[]{:S(2)}) collective-permute-start(f32[64,384]{1,0:T(8,128)S(1)} %get-tuple-element.30), channel_id=1, source_target_pairs={{0,32},{32,0},{1,33},{33,1},{2,34},{34,2},{3,35},{35,3},{4,36},{36... | collective-permute-start | bytes 294920 | tf_op jit(solution)/shard_map/ppermute | solution.py:259
  63.7 5.4 %collective-permute-start.4 = (f32[64,256]{1,0:T(8,128)S(1)}, f32[64,256]{1,0:T(8,128)S(1)}, u32[]{:S(2)}, u32[]{:S(2)}) collective-permute-start(f32[64,256]{1,0:T(8,128)S(1)} %slice.4), channel_id=1, source_target_pairs={{0,128},{64,192},{128,0},{192,64},{1,129},{65,193},{129,1},{193,65... | collective-permute-start | bytes 196616 | tf_op jit(solution)/shard_map/ppermute | solution.py:259
  64.4 4.7 %collective-permute-start.5 = (f32[64,256]{1,0:T(8,128)S(1)}, f32[64,256]{1,0:T(8,128)S(1)}, u32[]{:S(2)}, u32[]{:S(2)}) collective-permute-start(f32[64,256]{1,0:T(8,128)S(1)} %slice.4), channel_id=1, source_target_pairs={{0,192},{64,0},{128,64},{192,128},{1,193},{65,1},{129,65},{193,129... | collective-permute-start | bytes 196616 | tf_op jit(solution)/shard_map/ppermute | solution.py:259
  65.7 4.4 %collective-permute-start.3 = (f32[64,256]{1,0:T(8,128)S(1)}, f32[64,256]{1,0:T(8,128)S(1)}, u32[]{:S(2)}, u32[]{:S(2)}) collective-permute-start(f32[64,256]{1,0:T(8,128)S(1)} %slice.4), channel_id=1, source_target_pairs={{0,64},{64,128},{128,192},{192,0},{1,65},{65,129},{129,193},{193,1... | collective-permute-start | bytes 196616 | tf_op jit(solution)/shard_map/ppermute | solution.py:259
  109.0 6.5 %collective-permute-start.6 = (f32[16,64,128]{2,1,0:T(8,128)S(1)}, f32[16,64,128]{2,1,0:T(8,128)S(1)}, u32[]{:S(2)}, u32[]{:S(2)}) collective-permute-start(f32[16,64,128]{2,1,0:T(8,128)S(1)} %all_to_all.35.factor_ref.near_ref), channel_id=1, source_target_pairs={{0,32},{32,0},{1,33},{33,1},{2,34},{34,2},{3,35},{35,3},{4,36},{36... | collective-permute-start | bytes 1572872 | tf_op jit(solution)/shard_map/ppermute | solution.py:451
  116.6 1.3 %collective-permute-start.7 = (f32[64,256]{1,0:T(8,128)S(1)}, f32[64,256]{1,0:T(8,128)S(1)}, u32[]{:S(2)}, u32[]{:S(2)}) collective-permute-start(f32[64,256]{1,0:T(8,128)S(1)} %get-tuple-element.34.proj_ref), channel_id=1, source_target_pairs={{0,32},{32,0},{1,33},{33,1},{2,34},{34,2},{3,35},{35,3},{4,36},{36... | collective-permute-start | bytes 196616 | tf_op jit(solution)/shard_map/ppermute | solution.py:259
  118.0 5.0 %collective-permute-start.10 = (f32[64,256]{1,0:T(8,128)S(1)}, f32[64,256]{1,0:T(8,128)S(1)}, u32[]{:S(2)}, u32[]{:S(2)}) collective-permute-start(f32[64,256]{1,0:T(8,128)S(1)} %add.32.anchor_ref), channel_id=1, source_target_pairs={{0,192},{64,0},{128,64},{192,128},{1,193},{65,1},{129,65},{193,129... | collective-permute-start | bytes 196616 | tf_op jit(solution)/shard_map/ppermute | solution.py:259
  118.8 4.6 %collective-permute-start.9 = (f32[64,256]{1,0:T(8,128)S(1)}, f32[64,256]{1,0:T(8,128)S(1)}, u32[]{:S(2)}, u32[]{:S(2)}) collective-permute-start(f32[64,256]{1,0:T(8,128)S(1)} %add.32.anchor_ref), channel_id=1, source_target_pairs={{0,128},{64,192},{128,0},{192,64},{1,129},{65,193},{129,1},{193,65... | collective-permute-start | bytes 196616 | tf_op jit(solution)/shard_map/ppermute | solution.py:259
  119.5 5.8 %collective-permute-start.8 = (f32[64,256]{1,0:T(8,128)S(1)}, f32[64,256]{1,0:T(8,128)S(1)}, u32[]{:S(2)}, u32[]{:S(2)}) collective-permute-start(f32[64,256]{1,0:T(8,128)S(1)} %add.32.anchor_ref), channel_id=1, source_target_pairs={{0,64},{64,128},{128,192},{192,0},{1,65},{65,129},{129,193},{193,1... | collective-permute-start | bytes 196616 | tf_op jit(solution)/shard_map/ppermute | solution.py:259
  119.7 5.6 %copy-start = (f32[256,4096]{1,0:T(8,128)S(1)}, f32[256,4096]{1,0:T(8,128)}, u32[]{:S(2)}) copy-start(f32[256,4096]{1,0:T(8,128)} %momentum_ref.1) | copy-start | bytes 12582916
  119.7 5.6 %copy-start.1 = (bf16[256,4096]{1,0:T(8,128)(2,1)S(1)}, bf16[256,4096]{1,0:T(8,128)(2,1)}, u32[]{:S(2)}) copy-start(bf16[256,4096]{1,0:T(8,128)(2,1)} %weights_ref.1) | copy-start | bytes 6291460

commit v4 on v2

--- a/solution.py
+++ b/solution.py
@@ -62,12 +62,16 @@
     return core if own else 1 - core
 
 
-def merge_kernel(own, grad_ref, error_ref, basis_ref, anchor_ref, merged_ref, partial_ref, grads, errors, basis, sems):
+def merge_kernel(own, grad_ref, error_ref, basis_ref, other_ref, merged_ref, partial_ref, *refs):
     columns = grad_ref.shape[2]
     count = columns // 2 // CHUNK
     side = side_of(own)
+    grads, errors, basis, sems = refs[-4:]
     start = pltpu.make_async_copy(basis_ref, basis, sems.at[2, count])
     start.start()
+    if own:
+        leaving = pltpu.make_async_copy(other_ref, refs[0], sems.at[2, 0])
+        leaving.start()
     copies = []
     for c in range(count):
         here = slice(c * CHUNK, (c + 1) * CHUNK)
@@ -78,22 +82,18 @@
         for copy in pair:
             copy.start()
         copies.append(pair)
-    leaving = []
     start.wait()
     for c, pair in enumerate(copies):
         here = slice(c * CHUNK, (c + 1) * CHUNK)
         for copy in pair:
             copy.wait()
         merged = grads[:, here] + errors[:, here]
-        grads[:, here] = merged
-        copy = pltpu.make_async_copy(grads.at[:, here], merged_ref.at[:, here], sems.at[2, c])
-        copy.start()
-        leaving.append(copy)
+        merged_ref[:, here] = merged
         partial = rank_product(basis[...], *halves(merged))
         for j in range(CHUNK // LANES):
             partial_ref[c * (CHUNK // LANES) + j] = partial[:, j * LANES : (j + 1) * LANES]
-    for copy in leaving:
-        copy.wait()
+    if own:
+        leaving.wait()
 
 
 def partial_kernel(high_ref, low_ref, summed_ref, inverse_ref, partial_ref, basis_ref):
@@ -354,9 +354,13 @@
     half = columns // 2
     return flat_call(
         functools.partial(merge_kernel, own),
-        [IN_HBM] * 3 + [pl.BlockSpec(memory_space=pl.ANY)],
-        [pltpu.HBM((rows, half), F32), jax.ShapeDtypeStruct((half // LANES, ranks, LANES), F32)],
-        [IN_HBM, IN_VMEM],
+        [IN_HBM] * 3 + [IN_VMEM if own else pl.BlockSpec(memory_space=pl.ANY)],
+        [
+            jax.ShapeDtypeStruct((rows, half), F32),
+            jax.ShapeDtypeStruct((half // LANES, ranks, LANES), F32),
+        ]
+        + [pltpu.HBM((rows, half), F32)] * own,
+        [IN_VMEM, IN_VMEM] + [IN_HBM] * own,
         [
             pltpu.VMEM((rows, half), F32),
             pltpu.VMEM((rows, half), F32),
@@ -425,8 +429,8 @@
     square = whole(ranks, ranks)
     basis_t = warm_basis.T
 
-    away, given = merged_half(False, pseudo_grad, error_buffer, basis_t, basis_t)
-    kept, share = merged_half(True, pseudo_grad, error_buffer, basis_t, given)
+    other, given = merged_half(False, pseudo_grad, error_buffer, basis_t, basis_t)
+    kept, share, away = merged_half(True, pseudo_grad, error_buffer, basis_t, other)
     share = share + lax.ppermute(given, "core", SIBLING)
     share, leaving = lax.optimization_barrier((share, away))
     arrived = lax.ppermute(leaving, "core", SIBLING)

time: 132 us -> 131 us (level)
  no operation moved by 1% of the time
where the time goes in v4:
time: 131 us
  blocking collectives  83.4 us (64%)
  Pallas kernels  24.2 us (18%)
  starting transfers between devices  17 us (13%)
  waiting for transfers between devices  5.21 us (4%)
    all_to_all x4, blocking collectives, to_everyone(): return lax.all_to_all(copies, axes, 0, 0, tiled=True)  53.9 us
    all_to_all x2, blocking collectives, over_chips(): piece = lax.all_to_all(pieces, ('y', 'x'), 0, 0, tiled=True).sum(axis=0)  29.5 us
    ppermute x8, starting transfers between devices, summed_directly(): lax.ppermute(value, axis, around(axis, d))  8.69 us
    pallas_call x2, Pallas kernels, inverse_factor(): pl.pallas_call(inverse_kernel, grid=(1,), in_specs=[pl.BlockSpec((ranks,...  6.46 us
    pallas_call x2, Pallas kernels, merged_half(): flat_call(functools.partial(merge_kernel, own), [IN_HBM] * 3 + [IN_VMEM i...  5.96 us
    pallas_call x1, Pallas kernels, on_device(): flat_call(finish_kernel, [IN_VMEM] * 9, [pltpu.HBM((1, rows, columns), F3...  5.47 us
    ppermute x8, waiting for transfers between devices, summed_directly(): lax.ppermute(value, axis, around(axis, d))  5.2 us
    ppermute x1, starting transfers between devices, on_device(): far = lax.ppermute(near, 'core', SIBLING)  4.85 us
  transfers between devices with their start and end apart: 11, of which 5 were waited for; matrix products, arithmetic and copies ran while one was open for 0% of the time, Pallas kernels for 9%

profile of v4, /device:TPU:1, one launch (start us, length us, event | category | flops | bytes accessed | tf_op | source)
XLA Modules:
  0.0 131.1 jit_solution(7757332421814285610)
XLA Ops:
  0.6 2.6 %shard_map.84 = (f32[256,2048]{1,0:T(8,128)S(1)}, f32[16,64,128]{2,1,0:T(8,128)S(1)}) custom-call(f32[1,256,4096]{2,1,0:T(8,128)} %grad_ref.3, f32[1,256,4096]{2,1,0:T(8,128)} %error_ref.3, f32[64,256]{1,0:T(8,128)} %bitcast.2, f32[64,256]{1,0:T(8,128)} %bitcast.3), custom_call_target="tpu_custom_call" | custom-call | flops 201326592 | bytes 6291456 | tf_op jit(solution)/shard_map/pallas_call | solution.py:355
  3.2 3.3 %collective-permute-start = (f32[16,64,128]{2,1,0:T(8,128)S(1)}, f32[16,64,128]{2,1,0:T(8,128)S(1)}, u32[]{:S(2)}, u32[]{:S(2)}) collective-permute-start(f32[16,64,128]{2,1,0:T(8,128)S(1)} %get-tuple-element.26), channel_id=1, source_target_pairs={{0,32},{32,0},{1,33},{33,1},{2,34},{34,2},{3,35},{35,3},{4,36},{36... | collective-permute-start | bytes 1572872 | tf_op jit(solution)/shard_map/ppermute | solution.py:434
  6.6 3.4 %shard_map.85 = (f32[256,2048]{1,0:T(8,128)S(1)}, f32[16,64,128]{2,1,0:T(8,128)S(1)}, f32[256,2048]{1,0:T(8,128)}) custom-call(f32[1,256,4096]{2,1,0:T(8,128)} %grad_ref.3, f32[1,256,4096]{2,1,0:T(8,128)} %error_ref.3, f32[64,256]{1,0:T(8,128)} %bitcast.4, f32[256,2048]{1,0:T(8,128)S(1)} %get-tuple-element.23.other_ref), custom_call_target="tpu_custom_call" | custom-call | flops 201326592 | bytes 6291456 | tf_op jit(solution)/shard_map/pallas_call | solution.py:355
  9.9 0.1 add.27
  10.0 0.1 collective-permute-start.1
  10.1 15.4 %all_to_all.30 = f32[16,64,128]{2,1,0:T(8,128)S(1)} all-to-all(f32[16,64,128]{2,1,0:T(8,128)S(1)} %add.27), channel_id=1, replica_groups=mesh['y'=4,'core'=2,'x'=4,'z'=8] {'y','x'}, dimensions={0} | all-to-all | bytes 1048576 | tf_op jit(solution)/shard_map/all_to_all | solution.py:270
  25.6 17.4 %all_to_all.31 = f32[8,64,128]{2,1,0:T(8,128)S(1)} all-to-all(f32[8,64,128]{2,1,0:T(8,128)S(1)} %broadcast_in_dim.8), channel_id=1, replica_groups=mesh['y'=4,'core'=2,'x'=4,'z'=8] {'z'}, dimensions={0} | all-to-all | bytes 524288 | tf_op jit(solution)/shard_map/all_to_all | solution.py:266
  43.0 12.8 %all_to_all.32.factor_ref = f32[16,64,128]{2,1,0:T(8,128)S(1)} all-to-all(f32[16,64,128]{2,1,0:T(8,128)S(1)} %broadcast_in_dim.9), channel_id=1, replica_groups=mesh['y'=4,'core'=2,'x'=4,'z'=8] {'y','x'}, dimensions={0} | all-to-all | bytes 1048576 | tf_op jit(solution)/shard_map/all_to_all | solution.py:266
  55.8 2.6 %shard_map.86 = (f32[64,384]{1,0:T(8,128)S(1)}, bf16[256,2048]{1,0:T(8,128)(2,1)S(1)}, bf16[256,2048]{1,0:T(8,128)(2,1)S(1)}) custom-call(f32[16,64,128]{2,1,0:T(8,128)S(1)} %all_to_all.32.factor_ref, f32[256,2048]{1,0:T(8,128)S(1)} %get-tuple-element.24.kept_ref.merged_ref, f32[256,2048]{1,0:T(8,128)} %collective-permute-done.1.arrived_ref), custom_call_target="tpu_custom_call" | custom-call | flops 201326592 | bytes 6291456 | tf_op jit(solution)/shard_map/pallas_call | solution.py:379
  58.4 4.5 %collective-permute-start.2 = (f32[64,384]{1,0:T(8,128)S(1)}, f32[64,384]{1,0:T(8,128)S(1)}, u32[]{:S(2)}, u32[]{:S(2)}) collective-permute-start(f32[64,384]{1,0:T(8,128)S(1)} %get-tuple-element.32), channel_id=1, source_target_pairs={{0,32},{32,0},{1,33},{33,1},{2,34},{34,2},{3,35},{35,3},{4,36},{36... | collective-permute-start | bytes 294920 | tf_op jit(solution)/shard_map/ppermute | solution.py:256
  62.9 0.9 collective-permute-done.2
  63.9 0.7 collective-permute-start.4
  64.5 1.3 collective-permute-start.5
  65.8 0.2 collective-permute-start.3
  66.0 3.2 %shard_map.87.inverse_ref = f32[64,64]{1,0:T(8,128)S(1)} custom-call(f32[64,384]{1,0:T(8,128)S(1)} %add.28.gram_ref.anchor_ref, f32[64,384]{1,0:T(8,128)S(1)} %add.28.gram_ref.anchor_ref), custom_call_target="tpu_custom_call" | custom-call | flops 2000000000 | bytes 1048576 | tf_op jit(solution)/shard_map/pallas_call | solution.py:317
  69.2 0.9 collective-permute-done.3
  70.2 1.0 shard_map.88
  71.2 14.1 %all_to_all.33 = f32[16,64,128]{2,1,0:T(8,128)S(1)} all-to-all(f32[16,64,128]{2,1,0:T(8,128)S(1)} %shard_map.88), channel_id=1, replica_groups=mesh['y'=4,'core'=2,'x'=4,'z'=8] {'y','x'}, dimensions={0} | all-to-all | bytes 1048576 | tf_op jit(solution)/shard_map/all_to_all | solution.py:270
  85.3 11.8 %all_to_all.34 = f32[8,64,128]{2,1,0:T(8,128)S(1)} all-to-all(f32[8,64,128]{2,1,0:T(8,128)S(1)} %broadcast_in_dim.10), channel_id=1, replica_groups=mesh['y'=4,'core'=2,'x'=4,'z'=8] {'z'}, dimensions={0} | all-to-all | bytes 524288 | tf_op jit(solution)/shard_map/all_to_all | solution.py:266
  97.2 11.9 %all_to_all.35.factor_ref.near_ref = f32[16,64,128]{2,1,0:T(8,128)S(1)} all-to-all(f32[16,64,128]{2,1,0:T(8,128)S(1)} %broadcast_in_dim.11), channel_id=1, replica_groups=mesh['y'=4,'core'=2,'x'=4,'z'=8] {'y','x'}, dimensions={0} | all-to-all | bytes 1048576 | tf_op jit(solution)/shard_map/all_to_all | solution.py:266
  109.2 4.9 %collective-permute-start.6 = (f32[16,64,128]{2,1,0:T(8,128)S(1)}, f32[16,64,128]{2,1,0:T(8,128)S(1)}, u32[]{:S(2)}, u32[]{:S(2)}) collective-permute-start(f32[16,64,128]{2,1,0:T(8,128)S(1)} %all_to_all.35.factor_ref.near_ref), channel_id=1, source_target_pairs={{0,32},{32,0},{1,33},{33,1},{2,34},{34,2},{3,35},{35,3},{4,36},{36... | collective-permute-start | bytes 1572872 | tf_op jit(solution)/shard_map/ppermute | solution.py:451
  114.0 1.6 %shard_map.89 = (f32[64,256]{1,0:T(8,128)S(1)}, f32[64,64]{1,0:T(8,128)S(1)}, f32[256,2048]{1,0:T(8,128)S(1)}) custom-call(f32[16,64,128]{2,1,0:T(8,128)S(1)} %all_to_all.35.factor_ref.near_ref, f32[256,2048]{1,0:T(8,128)S(1)} %get-tuple-element.24.kept_ref.merged_ref, f32[256,2048]{1,0:T(8,128)} %get-tuple-element.29.away_ref), custom_call_target="tpu_custom_call" | custom-call | flops 201326592 | bytes 4194304 | tf_op jit(solution)/shard_map/pallas_call | solution.py:393
  115.6 1.1 shard_map.90
  116.8 0.4 collective-permute-start.7
  117.1 1.0 collective-permute-done.7
  118.1 0.8 collective-permute-start.10
  119.0 0.7 collective-permute-start.9
  119.7 0.2 collective-permute-start.8
  119.8 3.2 %shard_map.91.inverse_ref = f32[64,64]{1,0:T(8,128)S(1)} custom-call(f32[64,64]{1,0:T(8,128)S(1)} %get-tuple-element.37.gram_ref, f32[64,256]{1,0:T(8,128)S(1)} %add.32.anchor_ref), custom_call_target="tpu_custom_call" | custom-call | flops 2000000000 | bytes 1048576 | tf_op jit(solution)/shard_map/pallas_call | solution.py:317
  123.1 0.5 collective-permute-done.9
  123.6 1.8 %collective-permute-done.8 = f32[64,256]{1,0:T(8,128)S(1)} collective-permute-done((f32[64,256]{1,0:T(8,128)S(1)}, f32[64,256]{1,0:T(8,128)S(1)}, u32[]{:S(2)}, u32[]{:S(2)}) %collective-permute-start.8) | collective-permute-done | bytes 65568 | tf_op jit(solution)/shard_map/ppermute | solution.py:256
  125.5 5.5 %shard_map.92 = (f32[1,256,4096]{2,1,0:T(8,128)}, f32[256,4096]{1,0:T(8,128)}, bf16[256,4096]{1,0:T(8,128)(2,1)}, f32[64,256]{1,0:T(8,128)}) custom-call(f32[256,2048]{1,0:T(8,128)S(1)} %get-tuple-element.24.kept_ref.merged_ref, f32[256,2048]{1,0:T(8,128)S(1)} %get-tuple-element.33.merged_ref.away_ref, f32[16,64,128]{2,1,0:T(8,128)S(1)} %all_to_all.35.factor_ref.near_ref, ...), custom_call_target="tpu_custom_call" | custom-call | flops 805306368 | bytes 20971520 | tf_op jit(solution)/shard_map/pallas_call | solution.py:457
  (23 shorter events, 0.3 us)
Async XLA Ops:
  3.2 6.7 %collective-permute-start = (f32[16,64,128]{2,1,0:T(8,128)S(1)}, f32[16,64,128]{2,1,0:T(8,128)S(1)}, u32[]{:S(2)}, u32[]{:S(2)}) collective-permute-start(f32[16,64,128]{2,1,0:T(8,128)S(1)} %get-tuple-element.26), channel_id=1, source_target_pairs={{0,32},{32,0},{1,33},{33,1},{2,34},{34,2},{3,35},{35,3},{4,36},{36... | collective-permute-start | bytes 1572872 | tf_op jit(solution)/shard_map/ppermute | solution.py:434
  10.0 45.8 %collective-permute-start.1 = (f32[256,2048]{1,0:T(8,128)}, f32[256,2048]{1,0:T(8,128)}, u32[]{:S(2)}, u32[]{:S(2)}) collective-permute-start(f32[256,2048]{1,0:T(8,128)} %get-tuple-element.29.away_ref), channel_id=1, source_target_pairs={{0,32},{32,0},{1,33},{33,1},{2,34},{34,2},{3,35},{35,3},{4,36},{36... | collective-permute-start | bytes 6291464 | tf_op jit(solution)/shard_map/ppermute | solution.py:436
  58.4 5.4 %collective-permute-start.2 = (f32[64,384]{1,0:T(8,128)S(1)}, f32[64,384]{1,0:T(8,128)S(1)}, u32[]{:S(2)}, u32[]{:S(2)}) collective-permute-start(f32[64,384]{1,0:T(8,128)S(1)} %get-tuple-element.32), channel_id=1, source_target_pairs={{0,32},{32,0},{1,33},{33,1},{2,34},{34,2},{3,35},{35,3},{4,36},{36... | collective-permute-start | bytes 294920 | tf_op jit(solution)/shard_map/ppermute | solution.py:256
  63.9 5.4 %collective-permute-start.4 = (f32[64,256]{1,0:T(8,128)S(1)}, f32[64,256]{1,0:T(8,128)S(1)}, u32[]{:S(2)}, u32[]{:S(2)}) collective-permute-start(f32[64,256]{1,0:T(8,128)S(1)} %slice.4), channel_id=1, source_target_pairs={{0,128},{64,192},{128,0},{192,64},{1,129},{65,193},{129,1},{193,65... | collective-permute-start | bytes 196616 | tf_op jit(solution)/shard_map/ppermute | solution.py:256
  64.5 4.7 %collective-permute-start.5 = (f32[64,256]{1,0:T(8,128)S(1)}, f32[64,256]{1,0:T(8,128)S(1)}, u32[]{:S(2)}, u32[]{:S(2)}) collective-permute-start(f32[64,256]{1,0:T(8,128)S(1)} %slice.4), channel_id=1, source_target_pairs={{0,192},{64,0},{128,64},{192,128},{1,193},{65,1},{129,65},{193,129... | collective-permute-start | bytes 196616 | tf_op jit(solution)/shard_map/ppermute | solution.py:256
  65.8 4.3 %collective-permute-start.3 = (f32[64,256]{1,0:T(8,128)S(1)}, f32[64,256]{1,0:T(8,128)S(1)}, u32[]{:S(2)}, u32[]{:S(2)}) collective-permute-start(f32[64,256]{1,0:T(8,128)S(1)} %slice.4), channel_id=1, source_target_pairs={{0,64},{64,128},{128,192},{192,0},{1,65},{65,129},{129,193},{193,1... | collective-permute-start | bytes 196616 | tf_op jit(solution)/shard_map/ppermute | solution.py:256
  109.2 6.5 %collective-permute-start.6 = (f32[16,64,128]{2,1,0:T(8,128)S(1)}, f32[16,64,128]{2,1,0:T(8,128)S(1)}, u32[]{:S(2)}, u32[]{:S(2)}) collective-permute-start(f32[16,64,128]{2,1,0:T(8,128)S(1)} %all_to_all.35.factor_ref.near_ref), channel_id=1, source_target_pairs={{0,32},{32,0},{1,33},{33,1},{2,34},{34,2},{3,35},{35,3},{4,36},{36... | collective-permute-start | bytes 1572872 | tf_op jit(solution)/shard_map/ppermute | solution.py:451
  116.8 1.3 %collective-permute-start.7 = (f32[64,256]{1,0:T(8,128)S(1)}, f32[64,256]{1,0:T(8,128)S(1)}, u32[]{:S(2)}, u32[]{:S(2)}) collective-permute-start(f32[64,256]{1,0:T(8,128)S(1)} %get-tuple-element.36.proj_ref), channel_id=1, source_target_pairs={{0,32},{32,0},{1,33},{33,1},{2,34},{34,2},{3,35},{35,3},{4,36},{36... | collective-permute-start | bytes 196616 | tf_op jit(solution)/shard_map/ppermute | solution.py:256
  118.1 5.0 %collective-permute-start.10 = (f32[64,256]{1,0:T(8,128)S(1)}, f32[64,256]{1,0:T(8,128)S(1)}, u32[]{:S(2)}, u32[]{:S(2)}) collective-permute-start(f32[64,256]{1,0:T(8,128)S(1)} %add.32.anchor_ref), channel_id=1, source_target_pairs={{0,192},{64,0},{128,64},{192,128},{1,193},{65,1},{129,65},{193,129... | collective-permute-start | bytes 196616 | tf_op jit(solution)/shard_map/ppermute | solution.py:256
  119.0 4.6 %collective-permute-start.9 = (f32[64,256]{1,0:T(8,128)S(1)}, f32[64,256]{1,0:T(8,128)S(1)}, u32[]{:S(2)}, u32[]{:S(2)}) collective-permute-start(f32[64,256]{1,0:T(8,128)S(1)} %add.32.anchor_ref), channel_id=1, source_target_pairs={{0,128},{64,192},{128,0},{192,64},{1,129},{65,193},{129,1},{193,65... | collective-permute-start | bytes 196616 | tf_op jit(solution)/shard_map/ppermute | solution.py:256
  119.7 5.7 %collective-permute-start.8 = (f32[64,256]{1,0:T(8,128)S(1)}, f32[64,256]{1,0:T(8,128)S(1)}, u32[]{:S(2)}, u32[]{:S(2)}) collective-permute-start(f32[64,256]{1,0:T(8,128)S(1)} %add.32.anchor_ref), channel_id=1, source_target_pairs={{0,64},{64,128},{128,192},{192,0},{1,65},{65,129},{129,193},{193,1... | collective-permute-start | bytes 196616 | tf_op jit(solution)/shard_map/ppermute | solution.py:256
  119.8 5.6 %copy-start = (f32[256,4096]{1,0:T(8,128)S(1)}, f32[256,4096]{1,0:T(8,128)}, u32[]{:S(2)}) copy-start(f32[256,4096]{1,0:T(8,128)} %momentum_ref.1) | copy-start | bytes 12582916
  119.8 5.6 %copy-start.1 = (bf16[256,4096]{1,0:T(8,128)(2,1)S(1)}, bf16[256,4096]{1,0:T(8,128)(2,1)}, u32[]{:S(2)}) copy-start(bf16[256,4096]{1,0:T(8,128)(2,1)} %weights_ref.1) | copy-start | bytes 6291460
